TPU v7x, 128 devices: a whole 4x4x4 slice. The times are simulated.
128 devices in a mesh: brick: 4 (over y), dom: 32 (over z, x, core).
Axes of the slice: x: 4, y: 4, z: 4, core: 2. Of those that a mesh axis runs over, the one named last changes fastest.
Arguments:
- strain: bfloat16 [162, 294912], P(None, ('brick', 'dom')), may hold values from -3 to 3
- strain_rate: bfloat16 [162, 294912], P(None, ('brick', 'dom')), may hold values from -3 to 3
- part_map: int32 [2, 294912], P(None, ('brick', 'dom')), may hold values from 0 to 127, as said below
- brick_map: int32 [2, 294912], P(None, ('brick', 'dom')), may hold values from 0 to 127, as said below
- connectivity: int32 [27, 294912], P(None, ('brick', 'dom')), may hold values from 0 to 29240, as said below
- density: float32 [294912], P(('brick', 'dom')), may hold values from 0.3 to 3
- weight_in: bfloat16 [128, 6], replicated, may hold values from -2.5 to 2.5
- bias_in: float32 [128], replicated, may hold values from -3 to 3
- weight_mid: bfloat16 [128, 128], replicated, may hold values from -0.5 to 0.5
- bias_mid: float32 [128], replicated, may hold values from -3 to 3
- weight_out: float32 [128], replicated, may hold values from -1.5 to 1.5
- grad_operator: bfloat16 [81, 162], replicated, may hold values from -0.5 to 0.5
Outputs:
- stress: bfloat16 [162, 294912], P(None, ('brick', 'dom'))
- stress_rate: bfloat16 [162, 294912], P(None, ('brick', 'dom'))
- nodal_force: float32 [3, 3742848], P(None, ('brick', 'dom'))
Inputs may be any that keep to these rules, and one draw needn't show every extreme that they name: `part_map`: row 0 names the partition (device index over brick, then dom) that owns the element, row 1 its place among the elements that its device sends to that partition, below 32; no two elements of one device share a pair. Each device sends to 96 partitions: exactly 32 elements to half of them and 16 to the other half, and each partition receives exactly 2304 elements. `brick_map`: for element j of partition p, row 0 is the device of the brick layout that holds it and row 1 the place that this device's part_map gives it; every pair (device, place) that part_map sends to p appears exactly once among p's elements. `connectivity`: each partition's elements are the 9 x 256 x 1 quadratic hexahedra of a structured block, in an order drawn from the seed. Node (i, j, k), i < 19, j < 513, k < 3, has the number (i * 513 + j) * 3 + k, and row (u * 3 + w) * 3 + z of element (ex, ey) is node (2 ex + u, 2 ey + w, z). The plane i = 18 of a partition is the plane i = 0 of the next partition along dom in the same brick group.
All inputs are finite; a program needn't handle non-finite values.
Results may differ from a plain program's by a relative error of at most 0.0069.
Values may be sent and summed in bfloat16 or wider, within the bound.
A program may use at most 64 MiB of HBM per device.

v0:
```python
import jax
import jax.numpy as jnp
import numpy as np
from jax import lax
from jax.sharding import PartitionSpec as P

STRAIN = 6
GAUSS = 27
ELNODES = 27
SWEEPS = 3
ALONG = 9
ACROSS = 256


damping = 0.5


def passed_along(value, axis, steps):
    count = lax.axis_size(axis)
    leading, last = (max(0, -steps), min(count, count - steps))
    return lax.ppermute(value, axis, [(source, source + steps) for source in range(leading, last)])


def mass_table():
    profile = np.array([[2.0, 1.0, 0.0], [1.0, 4.0, 1.0], [0.0, 1.0, 2.0]]) / 6.0
    table = (
        profile[:, None, None, :, None, None]
        * profile[None, :, None, None, :, None]
        * profile[None, None, :, None, None, :]
    )
    return table.reshape(27, 27)


def respond(strain_point, rate_point, weight_in, bias_in, weight_mid, bias_mid, weight_out):
    columns = strain_point.shape[1]
    act_one = jnp.tanh(
        jnp.dot(weight_in, strain_point, preferred_element_type=jnp.float32) + bias_in[:, None]
    )
    slope_one = 1.0 - act_one * act_one
    tan_one = slope_one * jnp.dot(weight_in, rate_point, preferred_element_type=jnp.float32)
    joined = jnp.concatenate([act_one.astype(jnp.bfloat16), tan_one.astype(jnp.bfloat16)], axis=1)
    middle = jnp.dot(weight_mid, joined, preferred_element_type=jnp.float32)
    act_two = jnp.tanh(middle[:, :columns] + bias_mid[:, None])
    tan_two = middle[:, columns:]
    slope_two = 1.0 - act_two * act_two
    grad_two = weight_out[:, None] * slope_two
    curv_two = -2.0 * weight_out[:, None] * act_two * slope_two * tan_two
    joined_back = jnp.concatenate(
        [grad_two.astype(jnp.bfloat16), curv_two.astype(jnp.bfloat16)], axis=1
    )
    backward = jnp.dot(weight_mid.T, joined_back, preferred_element_type=jnp.float32)
    back_one = backward[:, :columns]
    back_tan = backward[:, columns:]
    delta_one = slope_one * back_one
    delta_tan = slope_one * back_tan - 2.0 * act_one * tan_one * back_one
    joined_delta = jnp.concatenate(
        [delta_one.astype(jnp.bfloat16), delta_tan.astype(jnp.bfloat16)], axis=1
    )
    result = jnp.dot(weight_in.T, joined_delta, preferred_element_type=jnp.float32)
    return (result[:, :columns].astype(jnp.bfloat16), result[:, columns:].astype(jnp.bfloat16))


def pointwise(strain, strain_rate, weight_in, bias_in, weight_mid, bias_mid, weight_out):
    columns = strain.shape[1]
    points = (strain.reshape(GAUSS, STRAIN, columns), strain_rate.reshape(GAUSS, STRAIN, columns))

    def one_point(point_pair):
        return respond(
            point_pair[0], point_pair[1], weight_in, bias_in, weight_mid, bias_mid, weight_out
        )

    stress, stress_rate = lax.map(one_point, points)
    return (stress.reshape(GAUSS * STRAIN, columns), stress_rate.reshape(GAUSS * STRAIN, columns))


def relayout(buffer, partitions, capacity):
    height = buffer.shape[0]
    exchanged = lax.all_to_all(
        buffer.reshape(height, partitions, capacity),
        ("brick", "dom"),
        split_axis=1,
        concat_axis=1,
        tiled=True,
    )
    return exchanged.reshape(height, partitions * capacity)


def select_cols(data, onehot):
    return jnp.dot(data, onehot, preferred_element_type=jnp.float32).astype(jnp.bfloat16)


def scatter_grid(values):
    height = values.shape[0]
    cube = values.reshape(height, 3, 3, 3, ALONG, ACROSS)
    total = None
    for upper in range(3):
        for middle in range(3):
            padded = lax.pad(
                cube[:, upper, middle],
                jnp.float32(0.0),
                ((0, 0, 0), (0, 0, 0), (upper, 2 - upper, 1), (middle, 2 - middle, 1)),
            )
            total = padded if total is None else total + padded
    return total


def read_grid(grid):
    height = grid.shape[0]
    pieces = []
    for upper in range(3):
        for middle in range(3):
            pieces.append(
                grid[:, :, upper : upper + 2 * ALONG - 1 : 2, middle : middle + 2 * ACROSS - 1 : 2]
            )
    return jnp.stack(pieces, axis=1).reshape(height, 27, ALONG, ACROSS)


def share_planes(grid):
    last_index = grid.shape[2] - 1
    from_left = passed_along(grid[:, :, last_index, :], "dom", 1)
    from_right = passed_along(grid[:, :, 0, :], "dom", -1)
    grid = grid.at[:, :, 0, :].add(from_left)
    return grid.at[:, :, last_index, :].add(from_right)


def per_device(
    strain,
    strain_rate,
    part_map,
    brick_map,
    connectivity,
    density,
    weight_in,
    bias_in,
    weight_mid,
    bias_mid,
    weight_out,
    grad_operator,
):
    elem_count = strain.shape[1]
    partitions = lax.axis_size("brick") * lax.axis_size("dom")
    capacity = 16 * elem_count // (9 * partitions)
    slot_count = partitions * capacity
    send_columns = part_map[0] * capacity + part_map[1]
    take_columns = brick_map[0] * capacity + brick_map[1]
    node_row = connectivity[0] // 3
    grid_index = node_row // (2 * ACROSS + 1) // 2 * ACROSS + node_row % (2 * ACROSS + 1) // 2
    take_sorted = jnp.zeros((elem_count,), jnp.int32).at[grid_index].set(take_columns)
    density_grid = (
        jnp.zeros((elem_count,), jnp.float32).at[grid_index].set(density).reshape(ALONG, ACROSS)
    )
    slot_iota = lax.broadcasted_iota(jnp.int32, (1, slot_count), 1)
    send_onehot = (send_columns[:, None] == slot_iota).astype(jnp.bfloat16)
    take_onehot = (slot_iota.reshape(slot_count, 1) == take_sorted[None, :]).astype(jnp.bfloat16)
    stress, stress_rate = pointwise(
        strain, strain_rate, weight_in, bias_in, weight_mid, bias_mid, weight_out
    )
    elem_force = jnp.dot(grad_operator, stress, preferred_element_type=jnp.float32).astype(
        jnp.bfloat16
    )
    outgoing = select_cols(elem_force, send_onehot)
    elem_grid = select_cols(relayout(outgoing, partitions, capacity), take_onehot)
    mass_ref = jnp.asarray(mass_table(), jnp.float32)
    values = elem_grid.astype(jnp.float32).reshape(3, ELNODES, ALONG, ACROSS)
    weight = (jnp.diagonal(mass_ref)[:, None, None] * density_grid[None])[None]
    stacked = share_planes(jnp.concatenate([scatter_grid(values), scatter_grid(weight)], axis=0))
    nodal_load = stacked[:3]
    diagonal = stacked[3:]
    nodal_force = damping * nodal_load / diagonal
    for iteration in range(SWEEPS - 1):
        gathered = read_grid(nodal_force)
        applied = (
            jnp.einsum("ab,dbxy->daxy", mass_ref, gathered, precision=lax.Precision.HIGHEST)
            * density_grid[None, None]
        )
        nodal_force = (
            nodal_force + damping * (nodal_load - share_planes(scatter_grid(applied))) / diagonal
        )
    result = jnp.transpose(nodal_force, (0, 2, 3, 1)).reshape(3, -1)
    return (stress, stress_rate, result)


def solution(mesh):
    return jax.shard_map(
        per_device,
        mesh=mesh,
        in_specs=(
            P(None, ("brick", "dom")),
            P(None, ("brick", "dom")),
            P(None, ("brick", "dom")),
            P(None, ("brick", "dom")),
            P(None, ("brick", "dom")),
            P(("brick", "dom")),
            P(),
            P(),
            P(),
            P(),
            P(),
            P(),
        ),
        out_specs=(P(None, ("brick", "dom")), P(None, ("brick", "dom")), P(None, ("brick", "dom"))),
        check_vma=False,
    )
```

profile of v0, /device:TPU:7, one launch (start us, length us, event | category | flops | bytes accessed | tf_op | source)
XLA Modules:
  0.0 530.2 jit_solution(11281187518916555717)
XLA Ops:
  3.7 98.4 %while.18 = (s32[]{:T(128)}, bf16[27,6,2304]{2,1,0:T(8,128)(2,1)}, bf16[27,6,2304]{2,1,0:T(8,128)(2,1)}, bf16[27,6,2304]{2,1,0:T(8,128)(2,1)S(1)}, bf16[128,6]{0...) while((s32[]{:T(128)}, bf16[27,6,2304]{2,1,0:T(8,128)(2,1)}, ...), condition=%wide.region_1.2_spmd, body=%wide.region_0.1_spmd.sunk | while | flops 330624128 | bytes 23925376 | solution.py:72
  103.5 7.2 %fusion.33 = bf16[81,4096]{1,0:T(8,128)(2,1)S(1)} fusion(s32[2304]{0:T(1024)S(1)} %add_reduce_fusion.1, bf16[162,2304]{1,0:T(8,128)(2,1)S(1)} %reshape.475, bf16[81,162]{0,1:T(8,128)(2,1)S(1)} %copy-done), kind=kOutput, calls=%fused_computation.55 | convolution fusion | flops 1599245568 | bytes 1445508 | tf_op jit(solution)/shard_map/dot_general | solution.py:89
  112.1 11.3 %all-to-all-start = ((bf16[81,128,32]{0,2,1:T(8,128)(2,1)}), bf16[81,128,32]{0,2,1:T(8,128)(2,1)S(1)}, u32[]{:S(2)}, u32[]{:S(2)}) async-start(bf16[81,128,32]{0,2,1:T(8,128)(2,1)} %bitcast.11), calls=%async_computation | async-start | bytes 2097152 | tf_op jit(solution)/shard_map/all_to_all | solution.py:78
  125.5 9.2 %scatter_custom_fusion.1 = f32[2304]{0:T(1024)S(1)} fusion(s32[2304]{0:T(1024)S(1)} %fusion.42, f32[2304]{0:T(1024)} %param.32, f32[]{:T(128)} %constant.212.clone.1), kind=kCustom, calls=%fused_computation.162 | custom fusion | bytes 9728 | tf_op jit(solution)/shard_map/scatter | solution.py:150
  134.7 9.0 %scatter_custom_fusion = s32[2304]{0:T(1024)S(1)} fusion(s32[2304]{0:T(1024)S(1)} %fusion.42, s32[2304]{0:T(1024)S(1)} %add_reduce_fusion, s32[]{:T(128)} %constant.203.clone.1), kind=kCustom, calls=%fused_computation.164 | custom fusion | bytes 9220 | tf_op jit(solution)/shard_map/scatter | solution.py:148
  157.0 7.1 %fusion.35 = f32[81,2304]{1,0:T(8,128)S(1)} fusion(bf16[81,4096]{0,1:T(8,128)(2,1)S(1)} %bitcast.269, s32[2304]{0:T(1024)S(1)} %scatter_custom_fusion), kind=kOutput, calls=%fused_computation.57 | convolution fusion | flops 1538634240 | bytes 1419264 | tf_op jit(solution)/shard_map/dot_general | solution.py:89
  165.1 4.4 pad.121
  169.5 4.5 pad.126
  174.0 4.3 pad.125
  178.3 4.3 pad.124
  182.6 6.0 %pad.123 = f32[3,3,19,513]{3,2,1,0:T(8,128)S(1)} pad(f32[3,3,9,256]{3,2,1,0:T(8,128)} %get-tuple-element.164, f32[]{:T(128)} %constant.212.clone.1), padding=0_0_0x0_0_0x1_1_1x0_2_1 | pad | bytes 433840 | tf_op jit(solution)/shard_map/pad | solution.py:98
  188.6 7.5 %pad.122 = f32[3,3,19,513]{3,2,1,0:T(8,128)} pad(f32[3,3,9,256]{3,2,1,0:T(8,128)} %get-tuple-element.165, f32[]{:T(128)} %constant.212.clone.1), padding=0_0_0x0_0_0x0_2_1x2_0_1 | pad | bytes 433840 | tf_op jit(solution)/shard_map/pad | solution.py:98
  196.1 6.3 %pad.120 = f32[3,3,19,513]{3,2,1,0:T(8,128)} pad(f32[3,3,9,256]{3,2,1,0:T(8,128)S(1)} %get-tuple-element.166, f32[]{:T(128)} %constant.212.clone.1), padding=0_0_0x0_0_0x0_2_1x0_2_1 | pad | bytes 433840 | tf_op jit(solution)/shard_map/pad | solution.py:98
  202.4 6.4 %pad.128 = f32[3,3,19,513]{3,2,1,0:T(8,128)} pad(f32[3,3,9,256]{3,2,1,0:T(8,128)S(1)} %get-tuple-element.167, f32[]{:T(128)} %constant.212.clone.1), padding=0_0_0x0_0_0x2_0_1x2_0_1 | pad | bytes 433840 | tf_op jit(solution)/shard_map/pad | solution.py:98
  208.7 6.4 %pad.127 = f32[3,3,19,513]{3,2,1,0:T(8,128)} pad(f32[3,3,9,256]{3,2,1,0:T(8,128)S(1)} %get-tuple-element.168, f32[]{:T(128)} %constant.212.clone.1), padding=0_0_0x0_0_0x2_0_1x1_1_1 | pad | bytes 433840 | tf_op jit(solution)/shard_map/pad | solution.py:98
  217.0 3.5 collective-permute-start
  224.8 4.6 collective-permute-done.1
  230.4 3.1 slice.413
  236.7 3.1 slice.411
  243.0 3.1 slice.409
  246.1 3.1 slice.408
  249.2 3.1 slice.407
  252.4 3.1 slice.406
  255.5 3.1 slice.405
  262.2 5.8 %pad.142 = f32[3,3,19,513]{3,1,0,2:T(4,128)S(1)} pad(f32[3,3,9,256]{3,1,0,2:T(4,128)S(1)} %get-tuple-element.204, f32[]{:T(128)} %constant.212.clone.1), padding=0_0_0x0_0_0x1_1_1x1_1_1 | pad | bytes 433840 | tf_op jit(solution)/shard_map/pad | solution.py:98
  268.1 6.3 %pad.144 = f32[3,3,19,513]{3,1,0,2:T(4,128)S(1)} pad(f32[3,3,9,256]{3,1,0,2:T(4,128)S(1)} %get-tuple-element.202, f32[]{:T(128)} %constant.212.clone.1), padding=0_0_0x0_0_0x2_0_1x0_2_1 | pad | bytes 433840 | tf_op jit(solution)/shard_map/pad | solution.py:98
  274.4 5.8 %pad.146 = f32[3,3,19,513]{3,1,0,2:T(4,128)S(1)} pad(f32[3,3,9,256]{3,1,0,2:T(4,128)S(1)} %get-tuple-element.200, f32[]{:T(128)} %constant.212.clone.1), padding=0_0_0x0_0_0x2_0_1x2_0_1 | pad | bytes 433840 | tf_op jit(solution)/shard_map/pad | solution.py:98
  280.2 5.8 %pad.138 = f32[3,3,19,513]{3,1,0,2:T(4,128)S(1)} pad(f32[3,3,9,256]{3,1,0,2:T(4,128)S(1)} %bitcast.273, f32[]{:T(128)} %constant.212.clone.1), padding=0_0_0x0_0_0x0_2_1x0_2_1 | pad | bytes 433840 | tf_op jit(solution)/shard_map/pad | solution.py:98
  287.8 15.1 %pad.140 = f32[3,3,19,513]{3,1,0,2:T(4,128)} pad(f32[3,3,9,256]{3,1,0,2:T(4,128)} %get-tuple-element.206, f32[]{:T(128)} %constant.212.clone.1), padding=0_0_0x0_0_0x0_2_1x2_0_1 | pad | bytes 433840 | tf_op jit(solution)/shard_map/pad | solution.py:98
  302.9 12.2 %pad.141 = f32[3,3,19,513]{3,1,0,2:T(4,128)} pad(f32[3,3,9,256]{3,1,0,2:T(4,128)S(1)} %get-tuple-element.205, f32[]{:T(128)} %constant.212.clone.1), padding=0_0_0x0_0_0x1_1_1x0_2_1 | pad | bytes 433840 | tf_op jit(solution)/shard_map/pad | solution.py:98
  315.0 12.1 %pad.143 = f32[3,3,19,513]{3,1,0,2:T(4,128)} pad(f32[3,3,9,256]{3,1,0,2:T(4,128)S(1)} %get-tuple-element.203, f32[]{:T(128)} %constant.212.clone.1), padding=0_0_0x0_0_0x1_1_1x2_0_1 | pad | bytes 433840 | tf_op jit(solution)/shard_map/pad | solution.py:98
  327.2 12.2 %pad.145 = f32[3,3,19,513]{3,1,0,2:T(4,128)} pad(f32[3,3,9,256]{3,1,0,2:T(4,128)S(1)} %get-tuple-element.201, f32[]{:T(128)} %constant.212.clone.1), padding=0_0_0x0_0_0x2_0_1x1_1_1 | pad | bytes 433840 | tf_op jit(solution)/shard_map/pad | solution.py:98
  339.3 12.1 %pad.139 = f32[3,3,19,513]{3,1,0,2:T(4,128)} pad(f32[3,3,9,256]{3,1,0,2:T(4,128)S(1)} %get-tuple-element.207, f32[]{:T(128)} %constant.212.clone.1), padding=0_0_0x0_0_0x0_2_1x1_1_1 | pad | bytes 433840 | tf_op jit(solution)/shard_map/pad | solution.py:98
  359.2 5.6 %collective-permute-done.3 = f32[3,3,513]{2,1,0:T(4,128)S(1)} collective-permute-done((f32[3,3,513]{2,1,0:T(4,128)S(1)}, f32[3,3,513]{2,1,0:T(4,128)S(1)}, u32[]{:S(2)}, u32[]{:S(2)}) %collective-permute-start.3) | collective-permute-done | bytes 18500 | tf_op jit(solution)/shard_map/ppermute | solution.py:21
  365.1 3.1 slice.434
  371.3 3.1 slice.432
  398.0 6.0 %pad.155 = f32[3,3,19,513]{3,1,0,2:T(4,128)S(1)} pad(f32[3,3,9,256]{3,1,0,2:T(4,128)S(1)} %bitcast.279, f32[]{:T(128)} %constant.212.clone.1), padding=0_0_0x0_0_0x2_0_1x2_0_1 | pad | bytes 433840 | tf_op jit(solution)/shard_map/pad | solution.py:98
  404.1 5.8 %pad.147 = f32[3,3,19,513]{3,1,0,2:T(4,128)S(1)} pad(f32[3,3,9,256]{3,1,0,2:T(4,128)S(1)} %bitcast.278, f32[]{:T(128)} %constant.212.clone.1), padding=0_0_0x0_0_0x0_2_1x0_2_1 | pad | bytes 433840 | tf_op jit(solution)/shard_map/pad | solution.py:98
  409.9 12.2 %pad.149 = f32[3,3,19,513]{3,1,0,2:T(4,128)} pad(f32[3,3,9,256]{3,1,0,2:T(4,128)S(1)} %bitcast.277, f32[]{:T(128)} %constant.212.clone.1), padding=0_0_0x0_0_0x0_2_1x2_0_1 | pad | bytes 433840 | tf_op jit(solution)/shard_map/pad | solution.py:98
  422.1 12.1 %pad.150 = f32[3,3,19,513]{3,1,0,2:T(4,128)} pad(f32[3,3,9,256]{3,1,0,2:T(4,128)S(1)} %bitcast.276, f32[]{:T(128)} %constant.212.clone.1), padding=0_0_0x0_0_0x1_1_1x0_2_1 | pad | bytes 433840 | tf_op jit(solution)/shard_map/pad | solution.py:98
  434.2 12.2 %pad.151 = f32[3,3,19,513]{3,1,0,2:T(4,128)} pad(f32[3,3,9,256]{3,1,0,2:T(4,128)S(1)} %bitcast.275, f32[]{:T(128)} %constant.212.clone.1), padding=0_0_0x0_0_0x1_1_1x1_1_1 | pad | bytes 433840 | tf_op jit(solution)/shard_map/pad | solution.py:98
  446.4 12.1 %pad.152 = f32[3,3,19,513]{3,1,0,2:T(4,128)} pad(f32[3,3,9,256]{3,1,0,2:T(4,128)S(1)} %bitcast.274, f32[]{:T(128)} %constant.212.clone.1), padding=0_0_0x0_0_0x1_1_1x2_0_1 | pad | bytes 433840 | tf_op jit(solution)/shard_map/pad | solution.py:98
  458.5 12.1 %pad.153 = f32[3,3,19,513]{3,1,0,2:T(4,128)} pad(f32[3,3,9,256]{3,1,0,2:T(4,128)S(1)} %bitcast.272, f32[]{:T(128)} %constant.212.clone.1), padding=0_0_0x0_0_0x2_0_1x0_2_1 | pad | bytes 433840 | tf_op jit(solution)/shard_map/pad | solution.py:98
  470.7 12.2 %pad.154 = f32[3,3,19,513]{3,1,0,2:T(4,128)} pad(f32[3,3,9,256]{3,1,0,2:T(4,128)S(1)} %bitcast.271, f32[]{:T(128)} %constant.212.clone.1), padding=0_0_0x0_0_0x2_0_1x1_1_1 | pad | bytes 433840 | tf_op jit(solution)/shard_map/pad | solution.py:98
  482.8 12.1 %pad.148 = f32[3,3,19,513]{3,1,0,2:T(4,128)} pad(f32[3,3,9,256]{3,1,0,2:T(4,128)S(1)} %bitcast.270, f32[]{:T(128)} %constant.212.clone.1), padding=0_0_0x0_0_0x0_2_1x1_1_1 | pad | bytes 433840 | tf_op jit(solution)/shard_map/pad | solution.py:98
  505.2 3.4 collective-permute-done.5
  508.9 9.3 %copy.164 = f32[3,19,513,3]{3,2,1,0:T(8,128)} copy(f32[3,19,513,3]{2,1,3,0:T(8,128)S(1)} %add_bitcast_fusion) | data formatting | bytes 701784 | tf_op jit(solution)/shard_map/transpose | solution.py:179
  518.1 11.9 %reshape.489 = f32[3,29241]{1,0:T(4,128)} reshape(f32[3,19,513,3]{3,2,1,0:T(8,128)} %copy.164) | data formatting | bytes 701784 | tf_op jit(solution)/shard_map/reshape | solution.py:179
  (413 shorter events, 182.7 us)
Async XLA Ops:
  0.6 102.9 %copy-start = (bf16[81,162]{0,1:T(8,128)(2,1)S(1)}, bf16[81,162]{0,1:T(8,128)(2,1)}, u32[]{:S(2)}) copy-start(bf16[81,162]{0,1:T(8,128)(2,1)} %param.38) | copy-start | bytes 78736
  0.6 2.2 copy-start.6
  2.9 0.8 copy-start.3
  2.9 0.8 copy-start.8
  2.9 0.7 copy-start.11
  2.9 0.7 copy-start.12
  3.0 0.7 copy-start.13
  103.5 7.2 %copy-start.7 = (bf16[162,2304]{1,0:T(8,128)(2,1)}, bf16[162,2304]{1,0:T(8,128)(2,1)S(1)}, u32[]{:S(2)}) copy-start(bf16[162,2304]{1,0:T(8,128)(2,1)S(1)} %reshape.475) | copy-start | bytes 2239492
  112.1 11.4 %copy-start.2 = (f32[27,27]{1,0:T(8,128)S(1)}, f32[27,27]{1,0:T(8,128)}, u32[]{:S(2)}) copy-start(f32[27,27]{1,0:T(8,128)} %constant.215.clone) | copy-start | bytes 8752
  112.1 22.6 %copy-start.10 = (s32[2,2304]{1,0:T(2,128)S(1)}, s32[2,2304]{1,0:T(2,128)}, u32[]{:S(2)}) copy-start(s32[2,2304]{1,0:T(2,128)} %param.30) | copy-start | bytes 55300
  112.1 45.0 %all-to-all-start = ((bf16[81,128,32]{0,2,1:T(8,128)(2,1)}), bf16[81,128,32]{0,2,1:T(8,128)(2,1)S(1)}, u32[]{:S(2)}, u32[]{:S(2)}) async-start(bf16[81,128,32]{0,2,1:T(8,128)(2,1)} %bitcast.11), calls=%async_computation | async-start | bytes 2097152 | tf_op jit(solution)/shard_map/all_to_all | solution.py:78
  217.0 4.4 collective-permute-start
  221.6 7.9 %collective-permute-start.1 = (f32[4,3,513]{2,0,1:T(4,128)S(1)}, f32[4,3,513]{2,0,1:T(4,128)S(1)}, u32[]{:S(2)}, u32[]{:S(2)}) collective-permute-start(f32[4,3,513]{2,0,1:T(4,128)S(1)} %bitcast.280), channel_id=1, source_target_pairs={{1,0},{2,1},{3,2},{4,3},{5,4},{6,5},{7,6},{8,7},{9,8},{10,9},{11,1... | collective-permute-start | bytes 73880 | tf_op jit(solution)/shard_map/ppermute | solution.py:21
  229.7 0.7 copy-start.4
  259.3 0.7 copy-start.9
  353.8 11.2 %copy-start.5 = (f32[3,19,513]{2,1,0:T(8,128)S(1)}, f32[3,19,513]{2,1,0:T(8,128)}, u32[]{:S(2)}) copy-start(f32[3,19,513]{2,1,0:T(8,128)} %copy-done.4) | copy-start | bytes 350896
  353.8 3.2 collective-permute-start.2
  357.0 7.7 %collective-permute-start.3 = (f32[3,3,513]{2,1,0:T(4,128)S(1)}, f32[3,3,513]{2,1,0:T(4,128)S(1)}, u32[]{:S(2)}, u32[]{:S(2)}) collective-permute-start(f32[3,3,513]{2,1,0:T(4,128)S(1)} %get-tuple-element.189), channel_id=1, source_target_pairs={{1,0},{2,1},{3,2},{4,3},{5,4},{6,5},{7,6},{8,7},{9,8},{10,9},{11,1... | collective-permute-start | bytes 55412 | tf_op jit(solution)/shard_map/ppermute | solution.py:21
  497.7 3.1 collective-permute-start.4
  500.9 7.7 %collective-permute-start.5 = (f32[3,3,513]{2,1,0:T(4,128)S(1)}, f32[3,3,513]{2,1,0:T(4,128)S(1)}, u32[]{:S(2)}, u32[]{:S(2)}) collective-permute-start(f32[3,3,513]{2,1,0:T(4,128)S(1)} %get-tuple-element.187), channel_id=1, source_target_pairs={{1,0},{2,1},{3,2},{4,3},{5,4},{6,5},{7,6},{8,7},{9,8},{10,9},{11,1... | collective-permute-start | bytes 55412 | tf_op jit(solution)/shard_map/ppermute | solution.py:21
  518.1 11.9 %copy-start.1 = (bf16[81,162]{0,1:T(8,128)(2,1)S(1)}, bf16[81,162]{0,1:T(8,128)(2,1)}, u32[]{:S(2)}) copy-start(bf16[81,162]{0,1:T(8,128)(2,1)} %param.38) | copy-start | bytes 78736
where the time goes:
time: 541 us; the launch traced here: 530 us
  local copies, waits for them, and re-layouts  378 us (70%)
  matrix products  73.5 us (14%)
  other arithmetic  32.6 us (6%)
  starting transfers between devices  26 us (5%)
  waiting for transfers between devices  16.9 us (3%)
    pad x36, local copies, waits for them, and re-layouts, scatter_grid(): lax.pad(cube[:, upper, middle], jnp.float32(0.0), ((0, 0, 0), (0, 0, 0),...  247 us
    slice x18, local copies, waits for them, and re-layouts, read_grid(): grid[:, :, upper:upper + 2 * ALONG - 1:2, middle:middle + 2 * ACROSS - 1:2]  56.2 us
    dynamic_update_slice x27, local copies, waits for them, and re-layouts, pointwise(): stress, stress_rate = lax.map(one_point, points)  17.8 us
    ppermute x6, waiting for transfers between devices, passed_along(): lax.ppermute(value, axis, [(source, source + steps) for source in range(l...  16.9 us
    ppermute x6, starting transfers between devices, passed_along(): lax.ppermute(value, axis, [(source, source + steps) for source in range(l...  14.6 us
    dot_general x2, matrix products, select_cols(): jnp.dot(data, onehot, preferred_element_type=jnp.float32)  14.3 us
    dot_general x27, matrix products, respond(): middle = jnp.dot(weight_mid, joined, preferred_element_type=jnp.float32)  12.8 us
    dot_general x27, matrix products, respond(): jnp.dot(weight_mid.T, joined_back, preferred_element_type=jnp.float32)  12.1 us
  transfers between devices with their start and end apart: 7, of which 6 were waited for; matrix products, arithmetic and copies ran while one was open for 7% of the time, Pallas kernels for 0%

commit v1 on v0

v1 whole, which is shorter than its diff:
```python
import functools

import jax
import jax.numpy as jnp
import numpy as np
from jax import lax
from jax.experimental import pallas as pl
from jax.experimental.pallas import tpu as pltpu
from jax.sharding import PartitionSpec as P

BF = jnp.bfloat16
F32 = jnp.float32
G = 27
VAR = 0

def dot(a,b): return jnp.dot(a,b,preferred_element_type=F32)
def dot_nt(a,b): return lax.dot_general(a,b,(((1,),(1,)),((),())),preferred_element_type=F32)

def consts():
    selx=np.zeros((432,162),np.float32); selv=np.zeros((432,162),np.float32); ones=np.zeros((432,1),np.float32)
    selo=np.zeros((162,216),np.float32)
    for g in range(27):
        for c in range(6):
            selx[g*16+c,g*6+c]=1; selv[g*16+8+c,g*6+c]=1; selo[g*6+c,g*8+c]=1
        for r in (6,7,14): ones[g*16+r]=1
    return selx,selv,ones,selo

def prep(weight_in,bias_in,weight_mid,bias_mid,weight_out,grad_operator):
    rp=lambda a: lax.reduce_precision(a,8,7)
    hi=rp(bias_in); r=bias_in-hi; lo=rp(r); lo2=(r-lo).astype(BF); hi=hi.astype(BF); lo=lo.astype(BF)
    z=lambda a,b: jnp.zeros((a,b),BF)
    top=jnp.concatenate([weight_in,hi[:,None],lo[:,None],z(128,6),lo2[:,None],z(128,1)],1)
    bot=jnp.concatenate([z(128,8),weight_in,z(128,2)],1)
    win2=jnp.concatenate([top,bot],0)
    wback=weight_mid.T
    wt=jnp.pad(weight_in.T,((0,2),(0,0)))
    selx,selv,ones,selo=consts()
    selo=jnp.asarray(selo,BF)
    g3=jnp.pad(grad_operator.reshape(3,27,162),((0,0),(0,5),(0,0))).reshape(96,162)
    gsel=dot(g3,selo).astype(BF)
    so=jnp.concatenate([selo,gsel,jnp.zeros((14,216),BF)],0)
    return (jnp.asarray(selx,BF),jnp.asarray(selv,BF),jnp.asarray(np.tile(ones,(1,128)),F32),win2,weight_mid,jnp.stack([bias_mid,weight_out],1),wback,wt,so)

def kernelA(C,U,steps,x_ref,v_ref,pm_ref,selx,selv,ones,win2,wmid,bmid,wback,wt,so,s_ref,r_ref,send_ref,x16,o1,o2,fs):
    step=pl.program_id(0)
    xx=dot(selx[...],x_ref[...])+dot(selv[...],v_ref[...])
    x16[...]=(xx+ones[:,0:1]).astype(BF)
    def one(g):
        xg=x16[pl.ds(pl.multiple_of(g*16,16),16),:]
        h=dot(win2[...],xg)
        act=jnp.tanh(h[:128]); slope=1.0-act*act; tan=slope*h[128:]
        if VAR&1:
            mm=dot(wmid[...],jnp.concatenate([act.astype(BF),tan.astype(BF)],1)); m1=mm[:,:C]; m2=mm[:,C:]
        else:
            m1=dot(wmid[...],act.astype(BF)); m2=dot(wmid[...],tan.astype(BF))
        act2=jnp.tanh(m1+bmid[:,0:1]); s2=bmid[:,1:2]*(1.0-act2*act2)
        b1=dot(wback[...],s2.astype(BF)); b2=dot(wback[...],(act2*s2*m2).astype(BF))
        d1=(slope*b1).astype(BF); d2=(slope*b2+act*tan*b1).astype(BF)
        gg=pl.ds(pl.multiple_of(g*8,8),8)
        o1[gg,:]=dot(wt[...],d1)
        o2[gg,:]=dot(wt[...],d2)*-2.0
    def body(i,c):
        for u in range(U): one(i*U+u)
        return c
    lax.fori_loop(0,G//U,body,0)
    o1b=o1[...].astype(BF); o2b=o2[...].astype(BF)
    so1=so[0:162,:]
    s_ref[...]=dot(so1,o1b).astype(BF)
    r_ref[...]=dot(so1,o2b).astype(BF)
    fcol=dot(so[162:258,:],o1b).astype(BF)
    fs[:,pl.ds(pl.multiple_of(step*C,128),C)]=fcol
    @pl.when(step==steps-1)
    def _():
        n=fs.shape[1]
        p=pm_ref[0:1,:]; r=pm_ref[1:2,:]
        hi=p*8+r//4; lo=r%4
        F=fs[...].astype(F32)
        mf=[]
        for d in range(3):
            for l in range(4):
                mf.append(jnp.where(lo==l,F[d*32:(d+1)*32],0.0).astype(BF))
        mf=jnp.concatenate(mf,0)
        for blk in range(2):
            io=lax.broadcasted_iota(jnp.int32,(512,n),0)+blk*512
            oh=jnp.where(io==hi,1.0,0.0).astype(BF)
            out=dot_nt(oh,mf).astype(BF)
            for d in range(3):
                send_ref[blk*64:(blk+1)*64,d]=out[:,d*128:(d+1)*128].reshape(64,8,128)

def callA(strain,rate,pm,pr,C=256,U=3):
    n=strain.shape[1]; steps=n//C
    full=lambda a: pl.BlockSpec(a.shape,lambda i:(0,)*a.ndim)
    col=pl.BlockSpec((162,C),lambda i:(0,i))
    return pl.pallas_call(functools.partial(kernelA,C,U,steps),
        out_shape=(jax.ShapeDtypeStruct((162,n),BF),jax.ShapeDtypeStruct((162,n),BF),jax.ShapeDtypeStruct((128,3,8,128),BF)),
        grid=(steps,),
        in_specs=[col,col,full(pm)]+[full(a) for a in pr],
        out_specs=(col,col,pl.BlockSpec((128,3,8,128),lambda i:(0,0,0,0))),
        scratch_shapes=[pltpu.VMEM((432,C),BF),pltpu.VMEM((216,C),F32),pltpu.VMEM((216,C),F32),pltpu.VMEM((96,n),BF)],
        compiler_params=pltpu.CompilerParams(vmem_limit_bytes=48<<20),
        name="pointwise_send",
        cost_estimate=pl.CostEstimate(flops=16*10**9,bytes_accessed=4*10**6,transcendentals=16*10**6),
    )(strain,rate,pm,*pr)

def kernelC(r_ref,bm_ref,conn_ref,dens_ref,eg_ref):
    n=2304
    c0=conn_ref[0:1,:].astype(F32)
    nr=jnp.floor((c0+0.5)*(1.0/3.0))
    ix=jnp.floor((nr+0.5)*(1.0/513.0))
    ey=(nr-ix*513.0)*0.5
    up=jnp.where(ey>=128.0,1.0,0.0)
    ghi=(ix+up).astype(jnp.int32); glo=(ey-128.0*up).astype(jnp.int32)
    dens=dens_ref[...]
    d1=dens.astype(BF).astype(F32); e=dens-d1
    d2=e.astype(BF).astype(F32); d3=e-d2
    v=jnp.concatenate([bm_ref[0:1,:].astype(F32),bm_ref[1:2,:].astype(F32),d1,d2,d3,jnp.zeros((3,n),F32)],0)
    vm=jnp.concatenate([jnp.where(ghi==h,v,0.0) for h in range(18)],0).astype(BF)
    ohl=jnp.where(lax.broadcasted_iota(jnp.int32,(128,n),0)==glo,1.0,0.0).astype(BF)
    o=dot_nt(vm,ohl)
    vs=jnp.concatenate([o[h*8:(h+1)*8,:] for h in range(18)],1)
    rr=vs[1:2,:]; rhi=jnp.floor(rr*0.25)
    hi=(vs[0:1,:]*8.0+rhi).astype(jnp.int32); lo=(rr-4.0*rhi).astype(jnp.int32)
    R=jnp.concatenate([r_ref[:,d].reshape(1024,128) for d in range(3)],1)
    N=768
    row=lax.broadcasted_iota(jnp.int32,(32,N),0)
    for k in range(n//N):
        sl=slice(k*N,(k+1)*N)
        oh=jnp.where(lax.broadcasted_iota(jnp.int32,(1024,N),0)==hi[:,sl],1.0,0.0).astype(BF)
        T=lax.dot_general(R,oh,(((0,),(0,)),((),())),preferred_element_type=F32)
        for d in range(3):
            acc=jnp.where(row==27,vs[2+d:3+d,sl],0.0)
            for l in range(4):
                acc=acc+jnp.where(lo[:,sl]==l,T[d*128+l*32:d*128+(l+1)*32],0.0)
            eg_ref[d*32:(d+1)*32,sl]=acc.astype(BF)

def callC(R,bm,conn,dens):
    n=2304
    full=lambda a: pl.BlockSpec(a.shape,lambda i:(0,)*a.ndim)
    return pl.pallas_call(kernelC,grid=(1,),out_shape=jax.ShapeDtypeStruct((96,n),BF),
      in_specs=[full(R),full(bm),pl.BlockSpec((8,n),lambda i:(0,0)),full(dens)],
      out_specs=pl.BlockSpec((96,n),lambda i:(0,0)),
      compiler_params=pltpu.CompilerParams(vmem_limit_bytes=48<<20),name="take")(R,bm,conn,dens)

def fe_consts():
    m=np.array([[2,1,0],[1,4,1],[0,1,2]],np.float64)
    def rowof(u,w,z,d): return (u*3+w)*16+z*3+d
    A=np.zeros((144,144)); S=np.zeros((144,96)); dg=np.ones((144,1)); Q=np.zeros((216,144))
    for u in range(3):
     for w in range(3):
      for z in range(3):
       for d in range(3):
        r=rowof(u,w,z,d)
        S[r,d*32+(u*3+w)*3+z]=1
        dg[r]=m[u,u]*m[w,w]*m[z,z]
        Q[((u*3+w)*3+z)*8+d,r]=1
        for u2 in range(3):
         for w2 in range(3):
          for z2 in range(3):
            A[r,rowof(u2,w2,z2,d)]=m[u,u2]*m[w,w2]*m[z,z2]
    nn=np.arange(768); j=nn//3; z=nn%3; src=((j%2)*3+z)*128+j//2
    return A,S,np.tile(dg,(1,128)),Q,src[None,:].astype(np.int32)

def kernelE(L,O,Rt,A,S,dg,Q,src,out_ref):
    ext=jnp.concatenate([L[...],O[...],Rt[...]],1)
    dens=(ext[27:28].astype(F32)+ext[59:60].astype(F32)+ext[91:92].astype(F32))*(1.0/216.0)
    def shl(x):
        n=x.shape[1]; y=pltpu.roll(x,n-1,1)
        i=lax.broadcasted_iota(jnp.int32,(1,n),1)&255
        return jnp.where(i==255,0.0,y)
    def shr(x):
        n=x.shape[1]; y=pltpu.roll(x,1,1)
        i=lax.broadcasted_iota(jnp.int32,(1,n),1)&255
        return jnp.where(i==0,0.0,y)
    def assemble(h):
        g=[h[16*q:16*q+16] for q in range(9)]
        for u in range(3):
            a0,a2=g[u*3],g[u*3+2]
            g[u*3]=a0+shr(a2); g[u*3+2]=a2+shl(a0)
        z=jnp.zeros((16,256),F32); n=h.shape[1]
        for w in range(3):
            b0,b2=g[w],g[6+w]
            g[w]=b0+jnp.concatenate([z,b2[:,:n-256]],1)
            g[6+w]=b2+jnp.concatenate([b0[:,256:],z],1)
        return jnp.concatenate(g,0)
    load=assemble(dot(S[...],ext))
    diag=assemble(dg[:,0:1]*dens)
    hinv=0.5/jnp.where(diag>0.0,diag,1.0)
    c=lambda x: x[:,256:x.shape[1]-256]
    load=c(load); hinv=c(hinv); dens=c(dens)
    f=load*hinv
    for it in range(2):
        fh=f.astype(BF); fl=(f-fh.astype(F32)).astype(BF)
        h=(dot(A[...],fh)+dot(A[...],fl))*dens
        s=assemble(h)
        f=c(f+(load-s)*hinv)
        load=c(load); hinv=c(hinv); dens=c(dens)
    fh=f.astype(BF); fl=(f-fh.astype(F32)).astype(BF)
    parts=[dot(Q[...],fh),dot(Q[...],fl)]
    P=jnp.where(lax.broadcasted_iota(jnp.int32,(768,768),0)==src[...],1.0,0.0).astype(BF)
    lhs=[]
    for half in range(2):
        for p in parts:
            rows=[]
            for i in range(19):
                u,ex=(i%2,i//2) if i<18 else (2,8)
                b=ex*256+half*128
                rows.append(jnp.concatenate([p[((u*3+w)*3+z)*8:((u*3+w)*3+z)*8+8,b:b+128] for w in range(2) for z in range(3)],1))
            lhs.append(jnp.concatenate(rows,0))
    Y=dot(jnp.concatenate(lhs,0).astype(BF),P)
    fs=parts[0]+parts[1]
    for i in range(19):
        u,ex=(i%2,i//2) if i<18 else (2,8)
        r=slice(8*i,8*i+8)
        h0=Y[0:152][r]+Y[152:304][r]; h1=Y[304:456][r]+Y[456:608][r]
        last=[fs[((u*3+2)*3+z)*8:((u*3+2)*3+z)*8+8,ex*256+255:ex*256+256] for z in range(3)]
        val=jnp.concatenate([h0,h1]+last,1)
        out_ref[:,i*1539:(i+1)*1539]=val[0:3]

def callE(L,O,Rt):
    A,S,dg,Q,src=fe_consts()
    ops=[L,O,Rt,jnp.asarray(A,BF),jnp.asarray(S,BF),jnp.asarray(dg,F32),jnp.asarray(Q,BF),jnp.asarray(src)]
    full=lambda a: pl.BlockSpec(a.shape,lambda i:(0,)*a.ndim)
    return pl.pallas_call(kernelE,grid=(1,),out_shape=jax.ShapeDtypeStruct((3,29241),F32),
      in_specs=[full(a) for a in ops],out_specs=pl.BlockSpec((3,29241),lambda i:(0,0)),
      compiler_params=pltpu.CompilerParams(vmem_limit_bytes=48<<20),name="project")(*ops)


def per_device(strain, strain_rate, part_map, brick_map, connectivity, density, *weights):
    stress, stress_rate, send = callA(strain, strain_rate, part_map, prep(*weights), 2304, 3)
    recv = lax.all_to_all(send, ("brick", "dom"), split_axis=0, concat_axis=0, tiled=True)
    grid = callC(recv, brick_map, connectivity, density.reshape(1, -1))
    count = lax.axis_size("dom")
    left = lax.ppermute(grid[:, 1536:], "dom", [(i, i + 1) for i in range(count - 1)])
    right = lax.ppermute(grid[:, :768], "dom", [(i + 1, i) for i in range(count - 1)])
    return stress, stress_rate, callE(left, grid, right)


def solution(mesh):
    split = P(None, ("brick", "dom"))
    return jax.shard_map(
        per_device,
        mesh=mesh,
        in_specs=(split,) * 5 + (P(("brick", "dom")),) + (P(),) * 6,
        out_specs=(split,) * 3,
        check_vma=False,
    )
```

time: 541 us -> 103 us (0.19); the launches traced: 530 us -> 103 us
  local copies, waits for them, and re-layouts: 378 us -> 7.07 us
  matrix products: 73.5 us -> 0.14 us
  Pallas kernels: 0 us -> 55.1 us
  other arithmetic: 32.6 us -> 0.79 us
  starting transfers between devices: 26 us -> 17.7 us
    pad x36 -> x2, local copies, waits for them, and re-layouts: 247 us -> 0.02 us  [the longest x1 0.01 us: prep(): jnp.pad(grad_operator.reshape(3, 27, 162), ((0, 0), (0, 5), (0, 0)))]
    dot_general x139 -> x1, matrix products: 73.5 us -> 0.14 us  [dot(): return jnp.dot(a, b, preferred_element_type=F32)]
    slice x21 -> x1, local copies, waits for them, and re-layouts: 57.2 us -> 0.02 us  [per_device(): grid[:, :768]]
    pallas_call x0 -> x3, Pallas kernels: none -> 55.1 us  [the longest x1 46.1 us: callA(): pl.pallas_call(functools.partial(kernelA, C, U, steps), out_shape=(jax.Sh...]
    convert_element_type x81 -> x0, other arithmetic: 22.8 us -> none  [the longest x27 10.8 us: respond(): grad_two.astype(jnp.bfloat16)]
    reshape x9 -> x2, local copies, waits for them, and re-layouts: 19.6 us -> 0.03 us  [the longest x1 0.03 us: prep(): grad_operator.reshape(3, 27, 162)]
    scatter x2 -> x0, local copies, waits for them, and re-layouts: 18.2 us -> none  [the longest x1 9.16 us: per_device(): jnp.zeros((elem_count,), jnp.float32).at[grid_index].set(density)]
    dynamic_update_slice x27 -> x0, local copies, waits for them, and re-layouts: 17.8 us -> none  [pointwise(): stress, stress_rate = lax.map(one_point, points)]
  transfers between devices with their start and end apart: 7 -> 3, of which waited for: 6 -> 2; matrix products, arithmetic and copies ran while one was open for 7% -> 0% of each run, Pallas kernels for 0% -> 0%
where the time goes in v1:
time: 103 us
  Pallas kernels  55.1 us (53%)
  waiting for transfers between devices  21 us (20%)
  starting transfers between devices  17.7 us (17%)
  local copies, waits for them, and re-layouts  7.07 us (7%)
    pallas_call x1, Pallas kernels, callA(): pl.pallas_call(functools.partial(kernelA, C, U, steps), out_shape=(jax.Sh...  46.1 us
    all_to_all x1, waiting for transfers between devices, per_device(): lax.all_to_all(send, ('brick', 'dom'), split_axis=0, concat_axis=0, tiled...  14.5 us
    all_to_all x1, starting transfers between devices, per_device(): lax.all_to_all(send, ('brick', 'dom'), split_axis=0, concat_axis=0, tiled...  10.8 us
    unnamed x42, local copies, waits for them, and re-layouts  6.61 us
    ppermute x1, waiting for transfers between devices, per_device(): lax.ppermute(grid[:, :768], 'dom', [(i + 1, i) for i in range(count - 1)])  6.45 us
    pallas_call x1, Pallas kernels, callE(): pl.pallas_call(kernelE, grid=(1,), out_shape=jax.ShapeDtypeStruct((3, 292...  6.17 us
    ppermute x1, starting transfers between devices, per_device(): lax.ppermute(grid[:, 1536:], 'dom', [(i, i + 1) for i in range(count - 1)])  4.76 us
    pallas_call x1, Pallas kernels, callC(): pl.pallas_call(kernelC, grid=(1,), out_shape=jax.ShapeDtypeStruct((96, n)...  2.84 us
  transfers between devices with their start and end apart: 3, of which 2 were waited for; matrix products, arithmetic and copies ran while one was open for 0% of the time, Pallas kernels for 0%

profile of v1, /device:TPU:7, one launch (start us, length us, event | category | flops | bytes accessed | tf_op | source)
XLA Modules:
  0.0 102.7 jit_solution(16449349679119168302)
XLA Ops:
  0.6 0.7 fusion.3
  1.3 0.7 copy-done.16
  2.0 0.1 concatenate.12
  2.0 0.0 copy-start.18
  2.1 0.0 copy-start.19
  2.1 0.0 copy-start.15
  2.1 0.0 copy-start.14
  2.1 0.1 copy.43.win2
  2.2 0.5 copy-done.18
  2.7 0.0 copy-done.19
  2.7 0.0 copy-start.8
  2.7 0.1 copy.44.bmid
  2.9 0.6 copy-done.5
  3.5 0.1 copy.41
  3.6 0.0 copy-done.15
  3.6 0.1 copy.42
  3.8 0.0 copy-done.14
  3.8 0.1 convolution_convert_fusion
  3.9 0.1 pad.12.clone
  4.0 0.1 maximum_maximum_fusion.so
  4.1 0.0 copy-done.8
  4.1 0.6 copy-done.10
  4.8 1.1 %copy-done.9 = bf16[162,2304]{1,0:T(8,128)(2,1)S(1)} copy-done((bf16[162,2304]{1,0:T(8,128)(2,1)S(1)}, bf16[162,2304]{1,0:T(8,128)(2,1)}, u32[]{:S(2)}) %copy-start.9) | copy-done | bytes 746520
  5.9 0.9 copy-done.11
  6.8 0.9 copy-done.12
  7.8 0.9 copy-done.13
  8.7 46.1 %pointwise_send.1 = (bf16[162,2304]{1,0:T(8,128)(2,1)}, bf16[162,2304]{1,0:T(8,128)(2,1)}, bf16[128,3,8,128]{3,2,1,0:T(8,128)(2,1)}) custom-call(bf16[162,2304]{1,0:T(8,128)(2,1)S(1)} %copy-done.8, bf16[162,2304]{1,0:T(8,128)(2,1)S(1)} %copy-done.9, s32[2,2304]{1,0:T(2,128)S(1)} %copy-done.10, bf16[432,162]{1,0:T(8,128)(2,1)S(1)} %copy-done.11, ...), custom_call_target="tpu_custom_call" | custom-call | flops 16000000000 | bytes 4000000 | tf_op jit(solution)/shard_map/pointwise_send/pallas_call | solution.py:94
  54.8 10.8 %all-to-all-start = ((bf16[128,3,8,128]{3,2,1,0:T(8,128)(2,1)}), bf16[128,3,8,128]{3,2,1,0:T(8,128)(2,1)S(1)}, u32[]{:S(2)}, u32[]{:S(2)}) async-start(bf16[128,3,8,128]{3,2,1,0:T(8,128)(2,1)} %get-tuple-element.8), calls=%async_computation | async-start | bytes 1572864 | tf_op jit(solution)/shard_map/all_to_all | solution.py:230
  65.6 0.0 copy-done.17
  65.6 0.0 copy-start.6
  65.6 14.5 %all-to-all-done.r_ref = bf16[128,3,8,128]{3,2,1,0:T(8,128)(2,1)S(1)} async-done(((bf16[128,3,8,128]{3,2,1,0:T(8,128)(2,1)}), bf16[128,3,8,128]{3,2,1,0:T(8,128)(2,1)S(1)}, u32[]{:S(2)}, u32[]{:S(2)}) %all-to-all-start) | async-done | bytes 786464 | tf_op jit(solution)/shard_map/all_to_all | solution.py:230
  80.2 0.0 copy-done
  80.2 0.0 copy-done.6
  80.2 2.8 %take.1.O = bf16[96,2304]{1,0:T(8,128)(2,1)S(1)} custom-call(bf16[128,3,8,128]{3,2,1,0:T(8,128)(2,1)S(1)} %all-to-all-done.r_ref, s32[2,2304]{1,0:T(2,128)S(1)} %copy-done.6, s32[27,2304]{1,0:T(8,128)S(1)} %copy-done, f32[1,2304]{1,0:T(1,128)S(1)} %reshape.17.dens_ref), custom_call_target="tpu_custom_call" | custom-call | tf_op jit(solution)/shard_map/take/pallas_call | solution.py:139
  83.0 0.0 copy-start.1
  83.0 0.0 copy-start.2
  83.0 0.0 copy-start.3
  83.1 0.0 copy-start.4
  83.1 0.0 copy-start.7
  83.1 4.8 %collective-permute-start = (bf16[96,768]{1,0:T(8,128)(2,1)S(1)}, bf16[96,768]{1,0:T(8,128)(2,1)S(1)}, u32[]{:S(2)}, u32[]{:S(2)}) collective-permute-start(bf16[96,768]{1,0:T(8,128)(2,1)S(1)} %get-tuple-element.10), channel_id=1, source_target_pairs={{0,1},{1,2},{2,3},{3,4},{4,5},{5,6},{6,7},{7,8},{8,9},{9,10},{10,1... | collective-permute-start | bytes 442376 | tf_op jit(solution)/shard_map/ppermute | solution.py:233
  87.9 2.1 %collective-permute-start.1 = (bf16[96,768]{1,0:T(8,128)(2,1)S(1)}, bf16[96,768]{1,0:T(8,128)(2,1)S(1)}, u32[]{:S(2)}, u32[]{:S(2)}) collective-permute-start(bf16[96,768]{1,0:T(8,128)(2,1)S(1)} %get-tuple-element.9), channel_id=1, source_target_pairs={{1,0},{2,1},{3,2},{4,3},{5,4},{6,5},{7,6},{8,7},{9,8},{10,9},{11,1... | collective-permute-start | bytes 442376 | tf_op jit(solution)/shard_map/ppermute | solution.py:234
  90.0 0.0 collective-permute-done.L
  90.0 6.5 %collective-permute-done.1.Rt = bf16[96,768]{1,0:T(8,128)(2,1)S(1)} collective-permute-done((bf16[96,768]{1,0:T(8,128)(2,1)S(1)}, bf16[96,768]{1,0:T(8,128)(2,1)S(1)}, u32[]{:S(2)}, u32[]{:S(2)}) %collective-permute-start.1) | collective-permute-done | bytes 147488 | tf_op jit(solution)/shard_map/ppermute | solution.py:234
  96.5 0.0 copy-done.1
  96.5 0.0 copy-done.2
  96.5 0.0 copy-done.3
  96.5 0.0 copy-done.4
  96.5 6.2 %project.1 = f32[3,29241]{1,0:T(4,128)} custom-call(bf16[96,768]{1,0:T(8,128)(2,1)S(1)} %collective-permute-done.L, bf16[96,2304]{1,0:T(8,128)(2,1)S(1)} %take.1.O, bf16[96,768]{1,0:T(8,128)(2,1)S(1)} %collective-permute-done.1.Rt, bf16[144,144]{1,0:T(8,128)(2,1)S(1)} %copy-done.2, bf16[144,96]{1,0:T(8,128)(2,1)S(1)} %copy-done.4, f32[144,128]{1,0:T(8,128)S(1)} %copy-done.3, ...), custom_call_target="tpu_custom_call" | custom-call | tf_op jit(solution)/shard_map/project/pallas_call | solution.py:223
  (22 shorter events, 0.1 us)
Async XLA Ops:
  1.3 0.7 copy-start.16
  2.0 0.7 copy-start.18
  2.1 0.7 copy-start.19
  2.1 1.5 %copy-start.15 = (bf16[81,162]{0,1:T(8,128)(2,1)S(1)}, bf16[81,162]{0,1:T(8,128)(2,1)}, u32[]{:S(2)}) copy-start(bf16[81,162]{0,1:T(8,128)(2,1)} %param.32) | copy-start | bytes 78736
  2.1 1.7 %copy-start.14 = (bf16[162,216]{1,0:T(8,128)(2,1)S(1)}, bf16[162,216]{1,0:T(8,128)(2,1)}, u32[]{:S(2)}) copy-start(bf16[162,216]{1,0:T(8,128)(2,1)} %constant.11.clone) | copy-start | bytes 209956
  2.7 0.8 copy-start.5
  2.7 1.4 %copy-start.8 = (bf16[162,2304]{1,0:T(8,128)(2,1)S(1)}, bf16[162,2304]{1,0:T(8,128)(2,1)}, u32[]{:S(2)}) copy-start(bf16[162,2304]{1,0:T(8,128)(2,1)} %x_ref.1) | copy-start | bytes 2239492
  4.0 0.7 copy-start.10
  4.7 1.1 %copy-start.9 = (bf16[162,2304]{1,0:T(8,128)(2,1)S(1)}, bf16[162,2304]{1,0:T(8,128)(2,1)}, u32[]{:S(2)}) copy-start(bf16[162,2304]{1,0:T(8,128)(2,1)} %v_ref.1) | copy-start | bytes 2239492
  5.9 0.9 copy-start.11
  6.8 0.9 copy-start.12
  7.8 0.9 copy-start.13
  54.8 10.8 %copy-start.17 = (f32[2304]{0:T(1024)S(1)}, f32[2304]{0:T(1024)}, u32[]{:S(2)}) copy-start(f32[2304]{0:T(1024)} %param.26) | copy-start | bytes 27652
  54.8 25.4 %copy-start = (s32[27,2304]{1,0:T(8,128)S(1)}, s32[27,2304]{1,0:T(8,128)}, u32[]{:S(2)}) copy-start(s32[27,2304]{1,0:T(8,128)} %conn_ref.1) | copy-start | bytes 746500
  54.8 25.4 %all-to-all-start = ((bf16[128,3,8,128]{3,2,1,0:T(8,128)(2,1)}), bf16[128,3,8,128]{3,2,1,0:T(8,128)(2,1)S(1)}, u32[]{:S(2)}, u32[]{:S(2)}) async-start(bf16[128,3,8,128]{3,2,1,0:T(8,128)(2,1)} %get-tuple-element.8), calls=%async_computation | async-start | bytes 1572864 | tf_op jit(solution)/shard_map/all_to_all | solution.py:230
  65.6 14.6 %copy-start.6 = (s32[2,2304]{1,0:T(2,128)S(1)}, s32[2,2304]{1,0:T(2,128)}, u32[]{:S(2)}) copy-start(s32[2,2304]{1,0:T(2,128)} %bm_ref.1) | copy-start | bytes 55300
  83.0 13.4 %copy-start.1 = (bf16[216,144]{1,0:T(8,128)(2,1)S(1)}, bf16[216,144]{1,0:T(8,128)(2,1)}, u32[]{:S(2)}) copy-start(bf16[216,144]{1,0:T(8,128)(2,1)} %constant.33.clone.Q) | copy-start | bytes 186628
  83.0 13.4 %copy-start.2 = (bf16[144,144]{1,0:T(8,128)(2,1)S(1)}, bf16[144,144]{1,0:T(8,128)(2,1)}, u32[]{:S(2)}) copy-start(bf16[144,144]{1,0:T(8,128)(2,1)} %constant.30.clone.A) | copy-start | bytes 124420
  83.0 13.4 %copy-start.3 = (f32[144,128]{1,0:T(8,128)S(1)}, f32[144,128]{1,0:T(8,128)}, u32[]{:S(2)}) copy-start(f32[144,128]{1,0:T(8,128)} %constant.32.clone.dg) | copy-start | bytes 221188
  83.1 13.4 %copy-start.4 = (bf16[144,96]{1,0:T(8,128)(2,1)S(1)}, bf16[144,96]{1,0:T(8,128)(2,1)}, u32[]{:S(2)}) copy-start(bf16[144,96]{1,0:T(8,128)(2,1)} %constant.31.clone.S) | copy-start | bytes 82948
  83.1 13.4 %copy-start.7 = (s32[1,768]{1,0:T(1,128)S(1)}, s32[1,768]{1,0:T(1,128)}, u32[]{:S(2)}) copy-start(s32[1,768]{1,0:T(1,128)} %constant.34.clone.src) | copy-start | bytes 9220
  83.1 6.9 %collective-permute-start = (bf16[96,768]{1,0:T(8,128)(2,1)S(1)}, bf16[96,768]{1,0:T(8,128)(2,1)S(1)}, u32[]{:S(2)}, u32[]{:S(2)}) collective-permute-start(bf16[96,768]{1,0:T(8,128)(2,1)S(1)} %get-tuple-element.10), channel_id=1, source_target_pairs={{0,1},{1,2},{2,3},{3,4},{4,5},{5,6},{6,7},{7,8},{8,9},{9,10},{10,1... | collective-permute-start | bytes 442376 | tf_op jit(solution)/shard_map/ppermute | solution.py:233
  87.9 8.6 %collective-permute-start.1 = (bf16[96,768]{1,0:T(8,128)(2,1)S(1)}, bf16[96,768]{1,0:T(8,128)(2,1)S(1)}, u32[]{:S(2)}, u32[]{:S(2)}) collective-permute-start(bf16[96,768]{1,0:T(8,128)(2,1)S(1)} %get-tuple-element.9), channel_id=1, source_target_pairs={{1,0},{2,1},{3,2},{4,3},{5,4},{6,5},{7,6},{8,7},{9,8},{10,9},{11,1... | collective-permute-start | bytes 442376 | tf_op jit(solution)/shard_map/ppermute | solution.py:234

commit v2 on v1

--- a/solution.py
+++ b/solution.py
@@ -8,99 +8,171 @@
 from jax.experimental.pallas import tpu as pltpu
 from jax.sharding import PartitionSpec as P
 
-BF = jnp.bfloat16
-F32 = jnp.float32
-G = 27
-VAR = 0
-
+BF=jnp.bfloat16; F32=jnp.float32
 def dot(a,b): return jnp.dot(a,b,preferred_element_type=F32)
 def dot_nt(a,b): return lax.dot_general(a,b,(((1,),(1,)),((),())),preferred_element_type=F32)
-
-def consts():
-    selx=np.zeros((432,162),np.float32); selv=np.zeros((432,162),np.float32); ones=np.zeros((432,1),np.float32)
-    selo=np.zeros((162,216),np.float32)
-    for g in range(27):
-        for c in range(6):
-            selx[g*16+c,g*6+c]=1; selv[g*16+8+c,g*6+c]=1; selo[g*6+c,g*8+c]=1
-        for r in (6,7,14): ones[g*16+r]=1
-    return selx,selv,ones,selo
-
-def prep(weight_in,bias_in,weight_mid,bias_mid,weight_out,grad_operator):
-    rp=lambda a: lax.reduce_precision(a,8,7)
-    hi=rp(bias_in); r=bias_in-hi; lo=rp(r); lo2=(r-lo).astype(BF); hi=hi.astype(BF); lo=lo.astype(BF)
-    z=lambda a,b: jnp.zeros((a,b),BF)
-    top=jnp.concatenate([weight_in,hi[:,None],lo[:,None],z(128,6),lo2[:,None],z(128,1)],1)
-    bot=jnp.concatenate([z(128,8),weight_in,z(128,2)],1)
-    win2=jnp.concatenate([top,bot],0)
-    wback=weight_mid.T
-    wt=jnp.pad(weight_in.T,((0,2),(0,0)))
-    selx,selv,ones,selo=consts()
-    selo=jnp.asarray(selo,BF)
-    g3=jnp.pad(grad_operator.reshape(3,27,162),((0,0),(0,5),(0,0))).reshape(96,162)
-    gsel=dot(g3,selo).astype(BF)
-    so=jnp.concatenate([selo,gsel,jnp.zeros((14,216),BF)],0)
-    return (jnp.asarray(selx,BF),jnp.asarray(selv,BF),jnp.asarray(np.tile(ones,(1,128)),F32),win2,weight_mid,jnp.stack([bias_mid,weight_out],1),wback,wt,so)
-
-def kernelA(C,U,steps,x_ref,v_ref,pm_ref,selx,selv,ones,win2,wmid,bmid,wback,wt,so,s_ref,r_ref,send_ref,x16,o1,o2,fs):
-    step=pl.program_id(0)
-    xx=dot(selx[...],x_ref[...])+dot(selv[...],v_ref[...])
-    x16[...]=(xx+ones[:,0:1]).astype(BF)
-    def one(g):
-        xg=x16[pl.ds(pl.multiple_of(g*16,16),16),:]
-        h=dot(win2[...],xg)
-        act=jnp.tanh(h[:128]); slope=1.0-act*act; tan=slope*h[128:]
-        if VAR&1:
-            mm=dot(wmid[...],jnp.concatenate([act.astype(BF),tan.astype(BF)],1)); m1=mm[:,:C]; m2=mm[:,C:]
-        else:
-            m1=dot(wmid[...],act.astype(BF)); m2=dot(wmid[...],tan.astype(BF))
-        act2=jnp.tanh(m1+bmid[:,0:1]); s2=bmid[:,1:2]*(1.0-act2*act2)
-        b1=dot(wback[...],s2.astype(BF)); b2=dot(wback[...],(act2*s2*m2).astype(BF))
-        d1=(slope*b1).astype(BF); d2=(slope*b2+act*tan*b1).astype(BF)
-        gg=pl.ds(pl.multiple_of(g*8,8),8)
-        o1[gg,:]=dot(wt[...],d1)
-        o2[gg,:]=dot(wt[...],d2)*-2.0
-    def body(i,c):
-        for u in range(U): one(i*U+u)
-        return c
-    lax.fori_loop(0,G//U,body,0)
-    o1b=o1[...].astype(BF); o2b=o2[...].astype(BF)
-    so1=so[0:162,:]
-    s_ref[...]=dot(so1,o1b).astype(BF)
-    r_ref[...]=dot(so1,o2b).astype(BF)
-    fcol=dot(so[162:258,:],o1b).astype(BF)
-    fs[:,pl.ds(pl.multiple_of(step*C,128),C)]=fcol
-    @pl.when(step==steps-1)
-    def _():
-        n=fs.shape[1]
-        p=pm_ref[0:1,:]; r=pm_ref[1:2,:]
-        hi=p*8+r//4; lo=r%4
-        F=fs[...].astype(F32)
-        mf=[]
-        for d in range(3):
-            for l in range(4):
-                mf.append(jnp.where(lo==l,F[d*32:(d+1)*32],0.0).astype(BF))
-        mf=jnp.concatenate(mf,0)
-        for blk in range(2):
-            io=lax.broadcasted_iota(jnp.int32,(512,n),0)+blk*512
-            oh=jnp.where(io==hi,1.0,0.0).astype(BF)
-            out=dot_nt(oh,mf).astype(BF)
-            for d in range(3):
-                send_ref[blk*64:(blk+1)*64,d]=out[:,d*128:(d+1)*128].reshape(64,8,128)
-
-def callA(strain,rate,pm,pr,C=256,U=3):
-    n=strain.shape[1]; steps=n//C
-    full=lambda a: pl.BlockSpec(a.shape,lambda i:(0,)*a.ndim)
-    col=pl.BlockSpec((162,C),lambda i:(0,i))
-    return pl.pallas_call(functools.partial(kernelA,C,U,steps),
-        out_shape=(jax.ShapeDtypeStruct((162,n),BF),jax.ShapeDtypeStruct((162,n),BF),jax.ShapeDtypeStruct((128,3,8,128),BF)),
-        grid=(steps,),
-        in_specs=[col,col,full(pm)]+[full(a) for a in pr],
-        out_specs=(col,col,pl.BlockSpec((128,3,8,128),lambda i:(0,0,0,0))),
-        scratch_shapes=[pltpu.VMEM((432,C),BF),pltpu.VMEM((216,C),F32),pltpu.VMEM((216,C),F32),pltpu.VMEM((96,n),BF)],
-        compiler_params=pltpu.CompilerParams(vmem_limit_bytes=48<<20),
-        name="pointwise_send",
-        cost_estimate=pl.CostEstimate(flops=16*10**9,bytes_accessed=4*10**6,transcendentals=16*10**6),
-    )(strain,rate,pm,*pr)
+MESH=pl.DeviceIdType.MESH
+EARLY=17
+U=1
+REMOTE=True
+
+
+def iota(shape, axis):
+    return lax.broadcasted_iota(jnp.int32, shape, axis)
+
+
+def ones_where(mask):
+    return jnp.where(mask, 1.0, 0.0).astype(BF)
+
+
+def pointwise_kernel(x_ref, v_ref, pm_ref, win_ref, bin_ref, wmid_ref, bmid_ref, wout_ref, grad_ref, s_ref, r_ref, recv_ref,
+                     x16, oo, bias, win2, wmid2, wback2, wt2, send, send_sem, recv_sem, own_sem):
+    n = x_ref.shape[1]
+    if REMOTE:
+        nb, nd = lax.axis_size("brick"), lax.axis_size("dom")
+        devices = nb * nd
+        b, d = lax.axis_index("brick"), lax.axis_index("dom")
+        me = b * nd + d
+        barrier = pltpu.get_barrier_semaphore()
+
+        def greet(k, carry):
+            t = lax.rem(me + k, devices)
+            pl.semaphore_signal(barrier, inc=1, device_id=(lax.div(t, nd), lax.rem(t, nd)), device_id_type=MESH)
+            return carry
+
+        lax.fori_loop(1, devices, greet, 0)
+
+    win = win_ref[...]
+    e16 = lambda k: ones_where(iota((6, 16), 1) == iota((6, 16), 0) + k)
+    win2[0:128] = dot(win, e16(0)).astype(BF)
+    win2[128:256] = dot(win, e16(8)).astype(BF)
+    wmid = wmid_ref[...]
+    zero = jnp.zeros((128, 128), BF)
+    wmid2[...] = jnp.concatenate([jnp.concatenate([wmid, zero], 1), jnp.concatenate([zero, wmid], 1)], 0)
+    back = wmid.astype(F32).T.astype(BF)
+    wback2[...] = jnp.concatenate([jnp.concatenate([back, zero], 1), jnp.concatenate([zero, back], 1)], 0)
+    e = lambda k: ones_where(iota((16, 6), 0) == iota((16, 6), 1) + k)
+    wt2[...] = jnp.concatenate([dot_nt(e(0), win).astype(BF), (-2.0 * dot_nt(e(8), win)).astype(BF)], 1)
+    for k, row in enumerate((bin_ref, bmid_ref, wout_ref)):
+        bias[k] = jnp.broadcast_to(row[...], (128, 128)).T
+
+    r, c = iota((432, 162), 0), iota((432, 162), 1)
+    first, place = lax.shift_right_logical(r, 4) * 6, r & 15
+    selx = ones_where((c == first + place) & (place < 6))
+    selv = ones_where((c == first + place - 8) & (place >= 8) & (place < 14))
+    for k in range(0, n, 768):
+        sl = slice(k, k + 768)
+        x16[:, sl] = (dot(selx, x_ref[:, sl]) + dot(selv, v_ref[:, sl])).astype(BF)
+
+    def column(k):
+        return jnp.concatenate([bias[k]] * (n // 128), 1)
+
+    def group(g):
+        return pl.ds(pl.multiple_of(g * 16, 16), 16)
+
+    def both(g):
+        h = dot(win2[...], x16[group(g), :])
+        act = jnp.tanh(h[:128] + column(0))
+        slope = 1.0 - act * act
+        tan = slope * h[128:]
+        m = dot(wmid2[...], jnp.concatenate([act.astype(BF), tan.astype(BF)], 0))
+        act2 = jnp.tanh(m[:128] + column(1))
+        grad = column(2) * (1.0 - act2 * act2)
+        bk = dot(wback2[...], jnp.concatenate([grad.astype(BF), (act2 * grad * m[128:]).astype(BF)], 0))
+        b1 = bk[:128]
+        d2 = slope * bk[128:] + act * tan * b1
+        oo[group(g), :] = dot(wt2[...], jnp.concatenate([(slope * b1).astype(BF), d2.astype(BF)], 0))
+
+    def value(g):
+        act = jnp.tanh(dot(win2[0:128], x16[group(g), :]) + column(0))
+        act2 = jnp.tanh(dot(wmid2[0:128, 0:128], act.astype(BF)) + column(1))
+        grad = column(2) * (1.0 - act2 * act2)
+        b1 = dot(wback2[0:128, 0:128], grad.astype(BF))
+        oo[group(g), :] = dot(wt2[:, 0:128], ((1.0 - act * act) * b1).astype(BF))
+
+    def run(body, low, high):
+        def step(i, carry):
+            for u in range(U):
+                body(low + i * U + u)
+            return carry
+        lax.fori_loop(0, (high - low) // U, step, 0)
+
+    run(both, 0, EARLY)
+    if EARLY < 27: run(value, EARLY, 27)
+
+    r, c = iota((162, 432), 0), iota((162, 432), 1)
+    first, place = lax.shift_right_logical(c, 4) * 6, c & 15
+    pick_s = ones_where((r == first + place) & (place < 6))
+    pick_r = ones_where((r == first + place - 8) & (place >= 8) & (place < 14))
+    r, c = iota((96, 81), 0), iota((96, 81), 1)
+    lane = r & 31
+    grad_op = dot(ones_where((c == lax.shift_right_logical(r, 5) * 27 + lane) & (lane < 27)), grad_ref[...]).astype(BF)
+    parts = []
+    for k in range(0, n, 768):
+        sl = slice(k, k + 768)
+        stress = dot(pick_s, oo[:, sl].astype(BF)).astype(BF)
+        s_ref[:, sl] = stress
+        parts.append(dot(grad_op, stress).astype(BF).astype(F32))
+    force = jnp.concatenate(parts, 1)
+    place = pm_ref[1:2, :]
+    high = pm_ref[0:1, :] * 8 + lax.shift_right_logical(place, 2)
+    low = place & 3
+    masked = jnp.concatenate(
+        [jnp.where(low == l, force[a * 32:(a + 1) * 32], 0.0).astype(BF) for a in range(3) for l in range(4)], 0)
+    for k in range(2):
+        onehot = ones_where(iota((512, n), 0) + k * 512 == high)
+        out = dot_nt(onehot, masked).astype(BF)
+        for a in range(3):
+            send[k * 64:(k + 1) * 64, a] = out[:, a * 128:(a + 1) * 128].reshape(64, 8, 128)
+
+    if REMOTE:
+        pl.semaphore_wait(barrier, devices - 1)
+        own = pltpu.make_async_copy(send.at[me], recv_ref.at[me], own_sem)
+        own.start()
+
+        def push(k, carry):
+            t = lax.rem(me + k, devices)
+            pltpu.make_async_remote_copy(
+                src_ref=send.at[t], dst_ref=recv_ref.at[me], send_sem=send_sem, recv_sem=recv_sem,
+                device_id=(lax.div(t, nd), lax.rem(t, nd)), device_id_type=MESH).start()
+            return carry
+
+        lax.fori_loop(1, devices, push, 0)
+
+    if EARLY < 27: run(both, EARLY, 27)
+    for k in range(0, n, 768):
+        sl = slice(k, k + 768)
+        r_ref[:, sl] = dot(pick_r, oo[:, sl].astype(BF)).astype(BF)
+
+    if REMOTE:
+        own.wait()
+        every = pltpu.make_async_remote_copy(
+            src_ref=send.at[pl.ds(0, devices - 1)], dst_ref=recv_ref.at[pl.ds(0, devices - 1)],
+            send_sem=send_sem, recv_sem=recv_sem, device_id=(b, d), device_id_type=MESH)
+        every.wait_send()
+        every.wait_recv()
+    else:
+        recv_ref[...] = send[...]
+
+
+def pointwise(strain, rate, part_map, weight_in, bias_in, weight_mid, bias_mid, weight_out, grad_operator):
+    n = strain.shape[1]
+    row = lambda a: a.reshape(1, 128)
+    out = jax.ShapeDtypeStruct((162, n), BF)
+    vmem = pl.BlockSpec(memory_space=pltpu.VMEM)
+    return pl.pallas_call(
+        pointwise_kernel,
+        out_shape=(out, out, jax.ShapeDtypeStruct((128, 3, 8, 128), BF)),
+        in_specs=[vmem] * 9,
+        out_specs=(vmem,) * 3,
+        scratch_shapes=[
+            pltpu.VMEM((432, n), BF), pltpu.VMEM((432, n), F32), pltpu.VMEM((3, 128, 128), F32), pltpu.VMEM((256, 16), BF),
+            pltpu.VMEM((256, 256), BF), pltpu.VMEM((256, 256), BF), pltpu.VMEM((16, 256), BF), pltpu.VMEM((128, 3, 8, 128), BF),
+            pltpu.SemaphoreType.DMA, pltpu.SemaphoreType.DMA, pltpu.SemaphoreType.DMA,
+        ],
+        compiler_params=pltpu.CompilerParams(vmem_limit_bytes=60 << 20, **(dict(collective_id=0, has_side_effects=True) if REMOTE else {})),
+        name="pointwise",
+    )(strain, rate, part_map, weight_in, row(bias_in), weight_mid, row(bias_mid), row(weight_out), grad_operator)
 
 def kernelC(r_ref,bm_ref,conn_ref,dens_ref,eg_ref):
     n=2304
@@ -139,7 +211,7 @@
     return pl.pallas_call(kernelC,grid=(1,),out_shape=jax.ShapeDtypeStruct((96,n),BF),
       in_specs=[full(R),full(bm),pl.BlockSpec((8,n),lambda i:(0,0)),full(dens)],
       out_specs=pl.BlockSpec((96,n),lambda i:(0,0)),
-      compiler_params=pltpu.CompilerParams(vmem_limit_bytes=48<<20),name="take")(R,bm,conn,dens)
+      compiler_params=pltpu.CompilerParams(vmem_limit_bytes=60<<20),name="take")(R,bm,conn,dens)
 
 def fe_consts():
     m=np.array([[2,1,0],[1,4,1],[0,1,2]],np.float64)
@@ -222,12 +294,11 @@
     full=lambda a: pl.BlockSpec(a.shape,lambda i:(0,)*a.ndim)
     return pl.pallas_call(kernelE,grid=(1,),out_shape=jax.ShapeDtypeStruct((3,29241),F32),
       in_specs=[full(a) for a in ops],out_specs=pl.BlockSpec((3,29241),lambda i:(0,0)),
-      compiler_params=pltpu.CompilerParams(vmem_limit_bytes=48<<20),name="project")(*ops)
+      compiler_params=pltpu.CompilerParams(vmem_limit_bytes=60<<20),name="project")(*ops)
 
 
 def per_device(strain, strain_rate, part_map, brick_map, connectivity, density, *weights):
-    stress, stress_rate, send = callA(strain, strain_rate, part_map, prep(*weights), 2304, 3)
-    recv = lax.all_to_all(send, ("brick", "dom"), split_axis=0, concat_axis=0, tiled=True)
+    stress, stress_rate, recv = pointwise(strain, strain_rate, part_map, *weights)
     grid = callC(recv, brick_map, connectivity, density.reshape(1, -1))
     count = lax.axis_size("dom")
     left = lax.ppermute(grid[:, 1536:], "dom", [(i, i + 1) for i in range(count - 1)])

time: 103 us -> 88.7 us (0.86)
  waiting for transfers between devices: 21 us -> 6.44 us
  Pallas kernels: 55.1 us -> 68.1 us
  starting transfers between devices: 17.7 us -> 6.28 us
    all_to_all x1 -> x0, waiting for transfers between devices: 14.5 us -> none  [per_device(): lax.all_to_all(send, ('brick', 'dom'), split_axis=0, concat_axis=0, tiled...]
    all_to_all x1 -> x0, starting transfers between devices: 10.8 us -> none  [per_device(): lax.all_to_all(send, ('brick', 'dom'), split_axis=0, concat_axis=0, tiled...]
    pallas_call x1, Pallas kernels: 46.1 us -> 56.1 us  [pointwise(): pl.pallas_call(pointwise_kernel, out_shape=(out, out, jax.ShapeDtypeStruc...]
    pallas_call x1, Pallas kernels: 2.84 us -> 4.75 us  [callC(): pl.pallas_call(kernelC, grid=(1,), out_shape=jax.ShapeDtypeStruct((96, n)...]
    unnamed x42 -> x16, local copies, waits for them, and re-layouts: 6.61 us -> 5.2 us
    pallas_call x1, Pallas kernels: 6.17 us -> 7.29 us  [callE(): pl.pallas_call(kernelE, grid=(1,), out_shape=jax.ShapeDtypeStruct((3, 292...]
  transfers between devices with their start and end apart: 3 -> 2, of which waited for: 2 -> 1; matrix products, arithmetic and copies ran while one was open for 0% -> 0% of each run, Pallas kernels for 0% -> 0%
where the time goes in v2:
time: 88.7 us; the launch traced here: 88.3 us
  Pallas kernels  68.1 us (77%)
  local copies, waits for them, and re-layouts  6.8 us (8%)
  waiting for transfers between devices  6.44 us (7%)
  starting transfers between devices  6.28 us (7%)
    pallas_call x1, Pallas kernels, pointwise(): pl.pallas_call(pointwise_kernel, out_shape=(out, out, jax.ShapeDtypeStruc...  56.1 us
    pallas_call x1, Pallas kernels, callE(): pl.pallas_call(kernelE, grid=(1,), out_shape=jax.ShapeDtypeStruct((3, 292...  7.29 us
    ppermute x1, waiting for transfers between devices, per_device(): lax.ppermute(grid[:, :768], 'dom', [(i + 1, i) for i in range(count - 1)])  6.44 us
    unnamed x16, local copies, waits for them, and re-layouts  5.2 us
    pallas_call x1, Pallas kernels, callC(): pl.pallas_call(kernelC, grid=(1,), out_shape=jax.ShapeDtypeStruct((96, n)...  4.75 us
    ppermute x1, starting transfers between devices, per_device(): lax.ppermute(grid[:, 1536:], 'dom', [(i, i + 1) for i in range(count - 1)])  4.18 us
    ppermute x1, starting transfers between devices, per_device(): lax.ppermute(grid[:, :768], 'dom', [(i + 1, i) for i in range(count - 1)])  2.1 us
  transfers between devices with their start and end apart: 2, of which 1 were waited for; matrix products, arithmetic and copies ran while one was open for 0% of the time, Pallas kernels for 0%

profile of v2, /device:TPU:7, one launch (start us, length us, event | category | flops | bytes accessed | tf_op | source)
XLA Modules:
  0.0 88.3 jit_solution(1028531423809454113)
XLA Ops:
  0.6 0.0 copy-start.5
  0.6 1.5 %copy.21.grad_ref = bf16[81,162]{1,0:T(8,128)(2,1)} copy(bf16[81,162]{0,1:T(8,128)(2,1)} %param.28) | data formatting | bytes 52488 | tf_op args[11]
  2.2 0.0 copy-done.5
  2.2 0.0 copy-start.4
  2.2 0.7 copy.20.win_ref
  2.9 0.0 copy-done.4
  2.9 0.6 reshape.21.dens_ref
  3.5 56.1 %pointwise.1 = (bf16[162,2304]{1,0:T(8,128)(2,1)}, bf16[162,2304]{1,0:T(8,128)(2,1)}, bf16[128,3,8,128]{3,2,1,0:T(8,128)(2,1)}) custom-call(bf16[162,2304]{1,0:T(8,128)(2,1)} %x_ref.1, bf16[162,2304]{1,0:T(8,128)(2,1)} %v_ref.1, s32[2,2304]{1,0:T(2,128)} %pm_ref.1, bf16[128,6]{1,0:T(8,128)(2,1)} %copy.20.win_ref, f32[1,128]{1,0:T(1,128)} %bitcast.3, ...), custom_call_target="tpu_custom_call" | custom-call | tf_op jit(solution)/shard_map/pointwise/pallas_call | solution.py:163
  59.6 4.7 %take.1.O = bf16[96,2304]{1,0:T(8,128)(2,1)} custom-call(bf16[128,3,8,128]{3,2,1,0:T(8,128)(2,1)} %get-tuple-element.8.r_ref, s32[2,2304]{1,0:T(2,128)} %bm_ref.1, s32[27,2304]{1,0:T(8,128)} %conn_ref.1, f32[1,2304]{1,0:T(1,128)} %reshape.21.dens_ref), custom_call_target="tpu_custom_call" | custom-call | tf_op jit(solution)/shard_map/take/pallas_call | solution.py:211
  64.3 1.0 %fusion = (bf16[96,768]{1,0:T(8,128)(2,1)S(1)}, bf16[96,768]{1,0:T(8,128)(2,1)S(1)}) fusion(bf16[96,2304]{1,0:T(8,128)(2,1)} %take.1.O), kind=kLoop, calls=%fused_computation | loop fusion | bytes 589824 | tf_op jit(solution)/shard_map/slice | solution.py:305
  65.3 0.0 copy-start.1
  65.3 4.2 %collective-permute-start = (bf16[96,768]{1,0:T(8,128)(2,1)S(1)}, bf16[96,768]{1,0:T(8,128)(2,1)S(1)}, u32[]{:S(2)}, u32[]{:S(2)}) collective-permute-start(bf16[96,768]{1,0:T(8,128)(2,1)S(1)} %get-tuple-element.10), channel_id=1, source_target_pairs={{0,1},{1,2},{2,3},{3,4},{4,5},{5,6},{6,7},{7,8},{8,9},{9,10},{10,1... | collective-permute-start | bytes 442376 | tf_op jit(solution)/shard_map/ppermute | solution.py:304
  69.5 2.1 %collective-permute-start.1 = (bf16[96,768]{1,0:T(8,128)(2,1)S(1)}, bf16[96,768]{1,0:T(8,128)(2,1)S(1)}, u32[]{:S(2)}, u32[]{:S(2)}) collective-permute-start(bf16[96,768]{1,0:T(8,128)(2,1)S(1)} %get-tuple-element.9), channel_id=1, source_target_pairs={{1,0},{2,1},{3,2},{4,3},{5,4},{6,5},{7,6},{8,7},{9,8},{10,9},{11,1... | collective-permute-start | bytes 442376 | tf_op jit(solution)/shard_map/ppermute | solution.py:305
  71.6 0.0 collective-permute-done.L
  71.6 0.0 copy-start.2
  71.7 6.4 %collective-permute-done.1.Rt = bf16[96,768]{1,0:T(8,128)(2,1)S(1)} collective-permute-done((bf16[96,768]{1,0:T(8,128)(2,1)S(1)}, bf16[96,768]{1,0:T(8,128)(2,1)S(1)}, u32[]{:S(2)}, u32[]{:S(2)}) %collective-permute-start.1) | collective-permute-done | bytes 147488 | tf_op jit(solution)/shard_map/ppermute | solution.py:305
  78.1 0.0 copy-done.2
  78.1 0.0 copy-start.3
  78.1 0.6 copy-done.3
  78.7 7.3 %project.1 = f32[3,29241]{1,0:T(4,128)} custom-call(bf16[96,768]{1,0:T(8,128)(2,1)} %copy-done.2, bf16[96,2304]{1,0:T(8,128)(2,1)} %take.1.O, bf16[96,768]{1,0:T(8,128)(2,1)} %copy-done.3, bf16[144,144]{1,0:T(8,128)(2,1)} %constant.10.clone.A, bf16[144,96]{1,0:T(8,128)(2,1)} %constant.11.clone.S, f32[144,128]{1,0:T(8,128)} %constant.12.clone.dg, ...), custom_call_target="tpu_custom_call" | custom-call | tf_op jit(solution)/shard_map/project/pallas_call | solution.py:295
  86.0 0.0 copy-done.1
  86.0 0.0 copy-start
  86.0 0.9 copy.24
  86.9 0.5 copy-done
  87.4 0.9 copy.25
Async XLA Ops:
  0.6 1.5 %copy-start.5 = (bf16[128,6]{0,1:T(8,128)(2,1)S(1)}, bf16[128,6]{0,1:T(8,128)(2,1)}, u32[]{:S(2)}) copy-start(bf16[128,6]{0,1:T(8,128)(2,1)} %param.23) | copy-start | bytes 4612
  2.2 0.7 copy-start.4
  65.3 20.7 %copy-start.1 = (bf16[162,2304]{1,0:T(8,128)(2,1)S(1)}, bf16[162,2304]{1,0:T(8,128)(2,1)}, u32[]{:S(2)}) copy-start(bf16[162,2304]{1,0:T(8,128)(2,1)} %get-tuple-element.14) | copy-start | bytes 2239492
  65.3 6.3 %collective-permute-start = (bf16[96,768]{1,0:T(8,128)(2,1)S(1)}, bf16[96,768]{1,0:T(8,128)(2,1)S(1)}, u32[]{:S(2)}, u32[]{:S(2)}) collective-permute-start(bf16[96,768]{1,0:T(8,128)(2,1)S(1)} %get-tuple-element.10), channel_id=1, source_target_pairs={{0,1},{1,2},{2,3},{3,4},{4,5},{5,6},{6,7},{7,8},{8,9},{9,10},{10,1... | collective-permute-start | bytes 442376 | tf_op jit(solution)/shard_map/ppermute | solution.py:304
  69.5 8.6 %collective-permute-start.1 = (bf16[96,768]{1,0:T(8,128)(2,1)S(1)}, bf16[96,768]{1,0:T(8,128)(2,1)S(1)}, u32[]{:S(2)}, u32[]{:S(2)}) collective-permute-start(bf16[96,768]{1,0:T(8,128)(2,1)S(1)} %get-tuple-element.9), channel_id=1, source_target_pairs={{1,0},{2,1},{3,2},{4,3},{5,4},{6,5},{7,6},{8,7},{9,8},{10,9},{11,1... | collective-permute-start | bytes 442376 | tf_op jit(solution)/shard_map/ppermute | solution.py:305
  71.6 6.5 %copy-start.2 = (bf16[96,768]{1,0:T(8,128)(2,1)}, bf16[96,768]{1,0:T(8,128)(2,1)S(1)}, u32[]{:S(2)}) copy-start(bf16[96,768]{1,0:T(8,128)(2,1)S(1)} %collective-permute-done.L) | copy-start | bytes 442372
  78.1 0.6 copy-start.3
  86.0 1.4 %copy-start = (bf16[162,2304]{1,0:T(8,128)(2,1)S(1)}, bf16[162,2304]{1,0:T(8,128)(2,1)}, u32[]{:S(2)}) copy-start(bf16[162,2304]{1,0:T(8,128)(2,1)} %get-tuple-element.15) | copy-start | bytes 2239492

commit v3 on v2

--- a/solution.py
+++ b/solution.py
@@ -25,8 +25,9 @@
     return jnp.where(mask, 1.0, 0.0).astype(BF)
 
 
-def pointwise_kernel(x_ref, v_ref, pm_ref, win_ref, bin_ref, wmid_ref, bmid_ref, wout_ref, grad_ref, s_ref, r_ref, recv_ref,
-                     x16, oo, bias, win2, wmid2, wback2, wt2, send, send_sem, recv_sem, own_sem):
+def pointwise_kernel(x_ref, v_ref, pm_ref, bm_ref, conn_ref, dens_ref, win_ref, bin_ref, wmid_ref, bmid_ref, wout_ref, grad_ref,
+                     s_out, r_out, grid_ref, left_ref, right_ref, s_ref, r_ref, x16, oo, bias, win2, wmid2, wback2, wt2, send,
+                     recv_ref, pick, send_sem, recv_sem, own_sem, s_sem, r_sem, left_send, left_recv, right_send, right_recv):
     n = x_ref.shape[1]
     if REMOTE:
         nb, nd = lax.axis_size("brick"), lax.axis_size("dom")
@@ -42,7 +43,7 @@
 
         lax.fori_loop(1, devices, greet, 0)
 
-    win = win_ref[...]
+    win = win_ref[...].astype(F32).T.astype(BF)
     e16 = lambda k: ones_where(iota((6, 16), 1) == iota((6, 16), 0) + k)
     win2[0:128] = dot(win, e16(0)).astype(BF)
     win2[128:256] = dot(win, e16(8)).astype(BF)
@@ -106,13 +107,15 @@
     pick_r = ones_where((r == first + place - 8) & (place >= 8) & (place < 14))
     r, c = iota((96, 81), 0), iota((96, 81), 1)
     lane = r & 31
-    grad_op = dot(ones_where((c == lax.shift_right_logical(r, 5) * 27 + lane) & (lane < 27)), grad_ref[...]).astype(BF)
+    grad_op = dot_nt(ones_where((c == lax.shift_right_logical(r, 5) * 27 + lane) & (lane < 27)), grad_ref[...]).astype(BF)
     parts = []
     for k in range(0, n, 768):
         sl = slice(k, k + 768)
         stress = dot(pick_s, oo[:, sl].astype(BF)).astype(BF)
         s_ref[:, sl] = stress
         parts.append(dot(grad_op, stress).astype(BF).astype(F32))
+    s_copy = pltpu.make_async_copy(s_ref, s_out, s_sem)
+    s_copy.start()
     force = jnp.concatenate(parts, 1)
     place = pm_ref[1:2, :]
     high = pm_ref[0:1, :] * 8 + lax.shift_right_logical(place, 2)
@@ -139,79 +142,112 @@
 
         lax.fori_loop(1, devices, push, 0)
 
-    if EARLY < 27: run(both, EARLY, 27)
+    run(both, EARLY, 27)
     for k in range(0, n, 768):
         sl = slice(k, k + 768)
         r_ref[:, sl] = dot(pick_r, oo[:, sl].astype(BF)).astype(BF)
-
-    if REMOTE:
-        own.wait()
-        every = pltpu.make_async_remote_copy(
-            src_ref=send.at[pl.ds(0, devices - 1)], dst_ref=recv_ref.at[pl.ds(0, devices - 1)],
-            send_sem=send_sem, recv_sem=recv_sem, device_id=(b, d), device_id_type=MESH)
-        every.wait_send()
-        every.wait_recv()
-    else:
-        recv_ref[...] = send[...]
-
-
-def pointwise(strain, rate, part_map, weight_in, bias_in, weight_mid, bias_mid, weight_out, grad_operator):
+    r_copy = pltpu.make_async_copy(r_ref, r_out, r_sem)
+    r_copy.start()
+
+    node = jnp.floor((conn_ref[0:1, :].astype(F32) + 0.5) * (1.0 / 3.0))
+    along = jnp.floor((node + 0.5) * (1.0 / 513.0))
+    across = (node - along * 513.0) * 0.5
+    half = jnp.where(across >= 128.0, 1.0, 0.0)
+    tile, lane = (along + half).astype(jnp.int32), (across - 128.0 * half).astype(jnp.int32)
+    density = dens_ref[...].reshape(1, n)
+    d1 = density.astype(BF).astype(F32)
+    d2 = (density - d1).astype(BF).astype(F32)
+    rows = jnp.concatenate(
+        [bm_ref[0:1, :].astype(F32), bm_ref[1:2, :].astype(F32), d1, d2, density - d1 - d2, jnp.zeros((3, n), F32)], 0)
+    tiles = n // 128
+    spread = jnp.concatenate([jnp.where(tile == t, rows, 0.0) for t in range(tiles)], 0).astype(BF)
+    sums = dot_nt(spread, ones_where(iota((128, n), 0) == lane))
+    sorted_rows = jnp.concatenate([sums[t * 8:(t + 1) * 8] for t in range(tiles)], 1)
+    place = sorted_rows[1:2]
+    place_high = jnp.floor(place * 0.25)
+    slot = (sorted_rows[0:1] * 8.0 + place_high).astype(jnp.int32)
+    low = (place - 4.0 * place_high).astype(jnp.int32)
+    for k in range(0, n, 768):
+        sl = slice(k, k + 768)
+        pick[:, sl] = ones_where(iota((1024, 768), 0) == slot[:, sl])
+
+    own.wait()
+    every = pltpu.make_async_remote_copy(
+        src_ref=send.at[pl.ds(0, devices - 1)], dst_ref=recv_ref.at[pl.ds(0, devices - 1)],
+        send_sem=send_sem, recv_sem=recv_sem, device_id=(b, d), device_id_type=MESH)
+    every.wait_send()
+    every.wait_recv()
+
+    slots = jnp.concatenate([recv_ref[:, a].reshape(1024, 128) for a in range(3)], 1)
+    line = iota((32, 768), 0)
+
+    def take(k):
+        sl = slice(k, k + 768)
+        found = lax.dot_general(slots, pick[:, sl], (((0,), (0,)), ((), ())), preferred_element_type=F32)
+        for a in range(3):
+            total = jnp.where(line == 27, sorted_rows[2 + a:3 + a, sl], 0.0)
+            for l in range(4):
+                total = total + jnp.where(low[:, sl] == l, found[a * 128 + l * 32:a * 128 + (l + 1) * 32], 0.0)
+            grid_ref[a * 32:(a + 1) * 32, sl] = total.astype(BF)
+
+    to_right = pltpu.make_async_remote_copy(
+        src_ref=grid_ref.at[:, pl.ds(n - 768, 768)], dst_ref=left_ref, send_sem=right_send, recv_sem=left_recv,
+        device_id=(b, lax.rem(d + 1, nd)), device_id_type=MESH)
+    to_left = pltpu.make_async_remote_copy(
+        src_ref=grid_ref.at[:, pl.ds(0, 768)], dst_ref=right_ref, send_sem=left_send, recv_sem=right_recv,
+        device_id=(b, lax.rem(d + nd - 1, nd)), device_id_type=MESH)
+    not_first, not_last = d > 0, d < nd - 1
+    take(0)
+    pl.when(not_first)(to_left.start)
+    take(n - 768)
+    pl.when(not_last)(to_right.start)
+    for k in range(768, n - 768, 768):
+        take(k)
+    s_copy.wait()
+    r_copy.wait()
+
+    @pl.when(not_first)
+    def _():
+        to_left.wait_send()
+        to_right.wait_recv()
+
+    @pl.when(not_last)
+    def _():
+        to_right.wait_send()
+        to_left.wait_recv()
+
+    @pl.when(d == 0)
+    def _():
+        left_ref[...] = jnp.zeros((96, 768), BF)
+
+    @pl.when(d == nd - 1)
+    def _():
+        right_ref[...] = jnp.zeros((96, 768), BF)
+
+
+def pointwise(strain, rate, part_map, brick_map, connectivity, density, weight_in, bias_in, weight_mid, bias_mid, weight_out,
+              grad_operator):
     n = strain.shape[1]
     row = lambda a: a.reshape(1, 128)
-    out = jax.ShapeDtypeStruct((162, n), BF)
+    points = jax.ShapeDtypeStruct((162, n), BF)
+    halo = jax.ShapeDtypeStruct((96, 768), BF)
     vmem = pl.BlockSpec(memory_space=pltpu.VMEM)
+    anywhere = pl.BlockSpec(memory_space=pl.ANY)
     return pl.pallas_call(
         pointwise_kernel,
-        out_shape=(out, out, jax.ShapeDtypeStruct((128, 3, 8, 128), BF)),
-        in_specs=[vmem] * 9,
-        out_specs=(vmem,) * 3,
+        out_shape=(points, points, jax.ShapeDtypeStruct((96, n), BF), halo, halo),
+        in_specs=[vmem] * 12,
+        out_specs=(anywhere,) * 2 + (vmem,) * 3,
         scratch_shapes=[
+            pltpu.VMEM((162, n), BF), pltpu.VMEM((162, n), BF),
             pltpu.VMEM((432, n), BF), pltpu.VMEM((432, n), F32), pltpu.VMEM((3, 128, 128), F32), pltpu.VMEM((256, 16), BF),
             pltpu.VMEM((256, 256), BF), pltpu.VMEM((256, 256), BF), pltpu.VMEM((16, 256), BF), pltpu.VMEM((128, 3, 8, 128), BF),
-            pltpu.SemaphoreType.DMA, pltpu.SemaphoreType.DMA, pltpu.SemaphoreType.DMA,
-        ],
-        compiler_params=pltpu.CompilerParams(vmem_limit_bytes=60 << 20, **(dict(collective_id=0, has_side_effects=True) if REMOTE else {})),
+            pltpu.VMEM((128, 3, 8, 128), BF), pltpu.VMEM((1024, n), BF),
+        ] + [pltpu.SemaphoreType.DMA] * 9,
+        compiler_params=pltpu.CompilerParams(vmem_limit_bytes=60 << 20, collective_id=0, has_side_effects=True),
         name="pointwise",
-    )(strain, rate, part_map, weight_in, row(bias_in), weight_mid, row(bias_mid), row(weight_out), grad_operator)
-
-def kernelC(r_ref,bm_ref,conn_ref,dens_ref,eg_ref):
-    n=2304
-    c0=conn_ref[0:1,:].astype(F32)
-    nr=jnp.floor((c0+0.5)*(1.0/3.0))
-    ix=jnp.floor((nr+0.5)*(1.0/513.0))
-    ey=(nr-ix*513.0)*0.5
-    up=jnp.where(ey>=128.0,1.0,0.0)
-    ghi=(ix+up).astype(jnp.int32); glo=(ey-128.0*up).astype(jnp.int32)
-    dens=dens_ref[...]
-    d1=dens.astype(BF).astype(F32); e=dens-d1
-    d2=e.astype(BF).astype(F32); d3=e-d2
-    v=jnp.concatenate([bm_ref[0:1,:].astype(F32),bm_ref[1:2,:].astype(F32),d1,d2,d3,jnp.zeros((3,n),F32)],0)
-    vm=jnp.concatenate([jnp.where(ghi==h,v,0.0) for h in range(18)],0).astype(BF)
-    ohl=jnp.where(lax.broadcasted_iota(jnp.int32,(128,n),0)==glo,1.0,0.0).astype(BF)
-    o=dot_nt(vm,ohl)
-    vs=jnp.concatenate([o[h*8:(h+1)*8,:] for h in range(18)],1)
-    rr=vs[1:2,:]; rhi=jnp.floor(rr*0.25)
-    hi=(vs[0:1,:]*8.0+rhi).astype(jnp.int32); lo=(rr-4.0*rhi).astype(jnp.int32)
-    R=jnp.concatenate([r_ref[:,d].reshape(1024,128) for d in range(3)],1)
-    N=768
-    row=lax.broadcasted_iota(jnp.int32,(32,N),0)
-    for k in range(n//N):
-        sl=slice(k*N,(k+1)*N)
-        oh=jnp.where(lax.broadcasted_iota(jnp.int32,(1024,N),0)==hi[:,sl],1.0,0.0).astype(BF)
-        T=lax.dot_general(R,oh,(((0,),(0,)),((),())),preferred_element_type=F32)
-        for d in range(3):
-            acc=jnp.where(row==27,vs[2+d:3+d,sl],0.0)
-            for l in range(4):
-                acc=acc+jnp.where(lo[:,sl]==l,T[d*128+l*32:d*128+(l+1)*32],0.0)
-            eg_ref[d*32:(d+1)*32,sl]=acc.astype(BF)
-
-def callC(R,bm,conn,dens):
-    n=2304
-    full=lambda a: pl.BlockSpec(a.shape,lambda i:(0,)*a.ndim)
-    return pl.pallas_call(kernelC,grid=(1,),out_shape=jax.ShapeDtypeStruct((96,n),BF),
-      in_specs=[full(R),full(bm),pl.BlockSpec((8,n),lambda i:(0,0)),full(dens)],
-      out_specs=pl.BlockSpec((96,n),lambda i:(0,0)),
-      compiler_params=pltpu.CompilerParams(vmem_limit_bytes=60<<20),name="take")(R,bm,conn,dens)
+    )(strain, rate, part_map, brick_map, connectivity, density, weight_in.T, row(bias_in), weight_mid, row(bias_mid), row(weight_out),
+      grad_operator.T)
 
 def fe_consts():
     m=np.array([[2,1,0],[1,4,1],[0,1,2]],np.float64)
@@ -232,7 +268,9 @@
     nn=np.arange(768); j=nn//3; z=nn%3; src=((j%2)*3+z)*128+j//2
     return A,S,np.tile(dg,(1,128)),Q,src[None,:].astype(np.int32)
 
-def kernelE(L,O,Rt,A,S,dg,Q,src,out_ref):
+def kernelE(s_in,r_in,L,O,Rt,A,S,dg,Q,src,s_out,r_out,out_ref,s_sem,r_sem):
+    s_copy=pltpu.make_async_copy(s_in,s_out,s_sem); r_copy=pltpu.make_async_copy(r_in,r_out,r_sem)
+    s_copy.start(); r_copy.start()
     ext=jnp.concatenate([L[...],O[...],Rt[...]],1)
     dens=(ext[27:28].astype(F32)+ext[59:60].astype(F32)+ext[91:92].astype(F32))*(1.0/216.0)
     def shl(x):
@@ -287,23 +325,22 @@
         last=[fs[((u*3+2)*3+z)*8:((u*3+2)*3+z)*8+8,ex*256+255:ex*256+256] for z in range(3)]
         val=jnp.concatenate([h0,h1]+last,1)
         out_ref[:,i*1539:(i+1)*1539]=val[0:3]
-
-def callE(L,O,Rt):
+    s_copy.wait(); r_copy.wait()
+
+def callE(s,r,L,O,Rt):
     A,S,dg,Q,src=fe_consts()
-    ops=[L,O,Rt,jnp.asarray(A,BF),jnp.asarray(S,BF),jnp.asarray(dg,F32),jnp.asarray(Q,BF),jnp.asarray(src)]
-    full=lambda a: pl.BlockSpec(a.shape,lambda i:(0,)*a.ndim)
-    return pl.pallas_call(kernelE,grid=(1,),out_shape=jax.ShapeDtypeStruct((3,29241),F32),
-      in_specs=[full(a) for a in ops],out_specs=pl.BlockSpec((3,29241),lambda i:(0,0)),
+    ops=[s,r,L,O,Rt,jnp.asarray(A,BF),jnp.asarray(S,BF),jnp.asarray(dg,F32),jnp.asarray(Q,BF),jnp.asarray(src)]
+    vmem=pl.BlockSpec(memory_space=pltpu.VMEM); anywhere=pl.BlockSpec(memory_space=pl.ANY)
+    point=jax.ShapeDtypeStruct(s.shape,BF)
+    return pl.pallas_call(kernelE,out_shape=(point,point,jax.ShapeDtypeStruct((3,29241),F32)),
+      in_specs=[anywhere]*2+[vmem]*(len(ops)-2),out_specs=(anywhere,anywhere,vmem),
+      scratch_shapes=[pltpu.SemaphoreType.DMA]*2,
       compiler_params=pltpu.CompilerParams(vmem_limit_bytes=60<<20),name="project")(*ops)
 
 
-def per_device(strain, strain_rate, part_map, brick_map, connectivity, density, *weights):
-    stress, stress_rate, recv = pointwise(strain, strain_rate, part_map, *weights)
-    grid = callC(recv, brick_map, connectivity, density.reshape(1, -1))
-    count = lax.axis_size("dom")
-    left = lax.ppermute(grid[:, 1536:], "dom", [(i, i + 1) for i in range(count - 1)])
-    right = lax.ppermute(grid[:, :768], "dom", [(i + 1, i) for i in range(count - 1)])
-    return stress, stress_rate, callE(left, grid, right)
+def per_device(*arguments):
+    stress, stress_rate, grid, left, right = pointwise(*arguments)
+    return callE(stress, stress_rate, left, grid, right)
 
 
 def solution(mesh):

time: 88.7 us -> 116 us (1.31); the launches traced: 88.3 us -> 114 us
  Pallas kernels: 68.1 us -> 114 us
  local copies, waits for them, and re-layouts: 6.8 us -> 0 us
  waiting for transfers between devices: 6.44 us -> 0 us
  starting transfers between devices: 6.28 us -> 0 us
    pallas_call x3 -> x2, Pallas kernels: 68.1 us -> 114 us  [the longest x1 63.6 us: pointwise(): pl.pallas_call(pointwise_kernel, out_shape=(points, points, jax.ShapeDtyp...]
    ppermute x2 -> x0, waiting for transfers between devices: 6.44 us -> none  [the longest x1 6.44 us: per_device(): lax.ppermute(grid[:, :768], 'dom', [(i + 1, i) for i in range(count - 1)])]
    ppermute x2 -> x0, starting transfers between devices: 6.28 us -> none  [the longest x1 4.18 us: per_device(): lax.ppermute(grid[:, 1536:], 'dom', [(i, i + 1) for i in range(count - 1)])]
    unnamed x16 -> x0, local copies, waits for them, and re-layouts: 5.2 us -> none
  transfers between devices with their start and end apart: 2 -> 0, of which waited for: 1 -> 0; matrix products, arithmetic and copies ran while one was open for 0% -> 0% of each run, Pallas kernels for 0% -> 0%
where the time goes in v3:
time: 116 us; the launch traced here: 114 us
  Pallas kernels  114 us (98%)
    pallas_call x1, Pallas kernels, pointwise(): pl.pallas_call(pointwise_kernel, out_shape=(points, points, jax.ShapeDtyp...  63.6 us
    pallas_call x1, Pallas kernels, callE(): pl.pallas_call(kernelE, out_shape=(point, point, jax.ShapeDtypeStruct((3,...  50 us

profile of v3, /device:TPU:7, one launch (start us, length us, event | category | flops | bytes accessed | tf_op | source)
XLA Modules:
  0.0 114.4 jit_solution(13011845148027330813)
XLA Ops:
  0.6 63.6 %pointwise.1 = (bf16[162,2304]{1,0:T(8,128)(2,1)}, bf16[162,2304]{1,0:T(8,128)(2,1)}, bf16[96,2304]{1,0:T(8,128)(2,1)}, bf16[96,768]{1,0:T(8,128)(2,1)}, bf16[96,768]{1,0:T(8,128)(2,1)}) custom-call(bf16[162,2304]{1,0:T(8,128)(2,1)} %x_ref.1, bf16[162,2304]{1,0:T(8,128)(2,1)} %v_ref.1, s32[2,2304]{1,0:T(2,128)} %pm_ref.1, s32[2,2304]{1,0:T(2,128)} %bm_ref.1, ...), custom_call_target="tpu_custom_call" | custom-call | tf_op jit(solution)/shard_map/pointwise/pallas_call | solution.py:236
  64.2 50.0 %project.1 = (bf16[162,2304]{1,0:T(8,128)(2,1)}, bf16[162,2304]{1,0:T(8,128)(2,1)}, f32[3,29241]{1,0:T(4,128)}) custom-call(bf16[162,2304]{1,0:T(8,128)(2,1)} %get-tuple-element.8.s_in, bf16[162,2304]{1,0:T(8,128)(2,1)} %get-tuple-element.9.r_in, bf16[96,768]{1,0:T(8,128)(2,1)} %get-tuple-element.10.L, bf16[96,2304]{1,0:T(8,128)(2,1)} %get-tuple-element.11.O, ...), custom_call_target="tpu_custom_call" | custom-call | tf_op jit(solution)/shard_map/project/pallas_call | solution.py:335

commit v4 on v3

--- a/solution.py
+++ b/solution.py
@@ -268,9 +268,10 @@
     nn=np.arange(768); j=nn//3; z=nn%3; src=((j%2)*3+z)*128+j//2
     return A,S,np.tile(dg,(1,128)),Q,src[None,:].astype(np.int32)
 
-def kernelE(s_in,r_in,L,O,Rt,A,S,dg,Q,src,s_out,r_out,out_ref,s_sem,r_sem):
-    s_copy=pltpu.make_async_copy(s_in,s_out,s_sem); r_copy=pltpu.make_async_copy(r_in,r_out,r_sem)
-    s_copy.start(); r_copy.start()
+def kernelE(s_in,r_in,L,O,Rt,A,S,dg,Q,src,s_out,r_out,out_ref,s_hold,r_hold,s_sem,r_sem):
+    load_s=pltpu.make_async_copy(s_in,s_hold,s_sem); load_r=pltpu.make_async_copy(r_in,r_hold,r_sem)
+    load_s.start(); load_r.start()
+    s_copy=pltpu.make_async_copy(s_hold,s_out,s_sem); r_copy=pltpu.make_async_copy(r_hold,r_out,r_sem)
     ext=jnp.concatenate([L[...],O[...],Rt[...]],1)
     dens=(ext[27:28].astype(F32)+ext[59:60].astype(F32)+ext[91:92].astype(F32))*(1.0/216.0)
     def shl(x):
@@ -297,6 +298,8 @@
     hinv=0.5/jnp.where(diag>0.0,diag,1.0)
     c=lambda x: x[:,256:x.shape[1]-256]
     load=c(load); hinv=c(hinv); dens=c(dens)
+    load_s.wait(); load_r.wait()
+    s_copy.start(); r_copy.start()
     f=load*hinv
     for it in range(2):
         fh=f.astype(BF); fl=(f-fh.astype(F32)).astype(BF)
@@ -334,7 +337,7 @@
     point=jax.ShapeDtypeStruct(s.shape,BF)
     return pl.pallas_call(kernelE,out_shape=(point,point,jax.ShapeDtypeStruct((3,29241),F32)),
       in_specs=[anywhere]*2+[vmem]*(len(ops)-2),out_specs=(anywhere,anywhere,vmem),
-      scratch_shapes=[pltpu.SemaphoreType.DMA]*2,
+      scratch_shapes=[pltpu.VMEM(s.shape,BF)]*2+[pltpu.SemaphoreType.DMA]*2,
       compiler_params=pltpu.CompilerParams(vmem_limit_bytes=60<<20),name="project")(*ops)
 
 

time: 116 us -> 73.5 us (0.63)
  Pallas kernels: 114 us -> 71.5 us
    pallas_call x1, Pallas kernels: 50 us -> 7.87 us  [callE(): pl.pallas_call(kernelE, out_shape=(point, point, jax.ShapeDtypeStruct((3,...]
where the time goes in v4:
time: 73.5 us; the launch traced here: 72.3 us
  Pallas kernels  71.5 us (97%)
  between operations  0.8 us (1%)
    pallas_call x1, Pallas kernels, pointwise(): pl.pallas_call(pointwise_kernel, out_shape=(points, points, jax.ShapeDtyp...  63.6 us
    pallas_call x1, Pallas kernels, callE(): pl.pallas_call(kernelE, out_shape=(point, point, jax.ShapeDtypeStruct((3,...  7.87 us

profile of v4, /device:TPU:7, one launch (start us, length us, event | category | flops | bytes accessed | tf_op | source)
XLA Modules:
  0.0 72.3 jit_solution(5144052514322544093)
XLA Ops:
  0.6 63.6 %pointwise.1 = (bf16[162,2304]{1,0:T(8,128)(2,1)}, bf16[162,2304]{1,0:T(8,128)(2,1)}, bf16[96,2304]{1,0:T(8,128)(2,1)}, bf16[96,768]{1,0:T(8,128)(2,1)}, bf16[96,768]{1,0:T(8,128)(2,1)}) custom-call(bf16[162,2304]{1,0:T(8,128)(2,1)} %x_ref.1, bf16[162,2304]{1,0:T(8,128)(2,1)} %v_ref.1, s32[2,2304]{1,0:T(2,128)} %pm_ref.1, s32[2,2304]{1,0:T(2,128)} %bm_ref.1, ...), custom_call_target="tpu_custom_call" | custom-call | tf_op jit(solution)/shard_map/pointwise/pallas_call | solution.py:236
  64.2 7.9 %project.1 = (bf16[162,2304]{1,0:T(8,128)(2,1)}, bf16[162,2304]{1,0:T(8,128)(2,1)}, f32[3,29241]{1,0:T(4,128)}) custom-call(bf16[162,2304]{1,0:T(8,128)(2,1)} %get-tuple-element.8.s_in, bf16[162,2304]{1,0:T(8,128)(2,1)} %get-tuple-element.9.r_in, bf16[96,768]{1,0:T(8,128)(2,1)} %get-tuple-element.10.L, bf16[96,2304]{1,0:T(8,128)(2,1)} %get-tuple-element.11.O, ...), custom_call_target="tpu_custom_call" | custom-call | tf_op jit(solution)/shard_map/project/pallas_call | solution.py:338

commit v5 on v4

--- a/solution.py
+++ b/solution.py
@@ -13,6 +13,7 @@
 def dot_nt(a,b): return lax.dot_general(a,b,(((1,),(1,)),((),())),preferred_element_type=F32)
 MESH=pl.DeviceIdType.MESH
 EARLY=17
+KEPT=7
 U=1
 REMOTE=True
 
@@ -27,7 +28,7 @@
 
 def pointwise_kernel(x_ref, v_ref, pm_ref, bm_ref, conn_ref, dens_ref, win_ref, bin_ref, wmid_ref, bmid_ref, wout_ref, grad_ref,
                      s_out, r_out, grid_ref, left_ref, right_ref, s_ref, r_ref, x16, oo, bias, win2, wmid2, wback2, wt2, send,
-                     recv_ref, pick, send_sem, recv_sem, own_sem, s_sem, r_sem, left_send, left_recv, right_send, right_recv):
+                     recv_ref, pick, keep, send_sem, recv_sem, own_sem, s_sem, r_sem, left_send, left_recv, right_send, right_recv):
     n = x_ref.shape[1]
     if REMOTE:
         nb, nd = lax.axis_size("brick"), lax.axis_size("dom")
@@ -91,6 +92,25 @@
         b1 = dot(wback2[0:128, 0:128], grad.astype(BF))
         oo[group(g), :] = dot(wt2[:, 0:128], ((1.0 - act * act) * b1).astype(BF))
 
+    def value_keep(g):
+        act = jnp.tanh(dot(win2[0:128], x16[group(g), :]) + column(0))
+        act2 = jnp.tanh(dot(wmid2[0:128, 0:128], act.astype(BF)) + column(1))
+        grad = column(2) * (1.0 - act2 * act2)
+        b1 = dot(wback2[0:128, 0:128], grad.astype(BF))
+        oo[group(g), :] = dot(wt2[:, 0:128], ((1.0 - act * act) * b1).astype(BF))
+        keep[g - EARLY, 0] = act
+        keep[g - EARLY, 1] = act2 * grad
+        keep[g - EARLY, 2] = b1
+
+    def rate(g):
+        act = keep[g - EARLY, 0]
+        slope = 1.0 - act * act
+        tan = slope * dot(win2[128:256], x16[group(g), :])
+        curv = keep[g - EARLY, 1] * dot(wmid2[0:128, 0:128], tan.astype(BF))
+        b2 = dot(wback2[0:128, 0:128], curv.astype(BF))
+        d2 = slope * b2 + act * tan * keep[g - EARLY, 2]
+        oo[pl.ds(pl.multiple_of(g * 16 + 8, 8), 8), :] = dot(wt2[:, 128:256], d2.astype(BF))[8:16]
+
     def run(body, low, high):
         def step(i, carry):
             for u in range(U):
@@ -99,7 +119,8 @@
         lax.fori_loop(0, (high - low) // U, step, 0)
 
     run(both, 0, EARLY)
-    if EARLY < 27: run(value, EARLY, 27)
+    run(value_keep, EARLY, EARLY + KEPT)
+    run(value, EARLY + KEPT, 27)
 
     r, c = iota((162, 432), 0), iota((162, 432), 1)
     first, place = lax.shift_right_logical(c, 4) * 6, c & 15
@@ -142,7 +163,8 @@
 
         lax.fori_loop(1, devices, push, 0)
 
-    run(both, EARLY, 27)
+    run(rate, EARLY, EARLY + KEPT)
+    run(both, EARLY + KEPT, 27)
     for k in range(0, n, 768):
         sl = slice(k, k + 768)
         r_ref[:, sl] = dot(pick_r, oo[:, sl].astype(BF)).astype(BF)
@@ -242,7 +264,7 @@
             pltpu.VMEM((162, n), BF), pltpu.VMEM((162, n), BF),
             pltpu.VMEM((432, n), BF), pltpu.VMEM((432, n), F32), pltpu.VMEM((3, 128, 128), F32), pltpu.VMEM((256, 16), BF),
             pltpu.VMEM((256, 256), BF), pltpu.VMEM((256, 256), BF), pltpu.VMEM((16, 256), BF), pltpu.VMEM((128, 3, 8, 128), BF),
-            pltpu.VMEM((128, 3, 8, 128), BF), pltpu.VMEM((1024, n), BF),
+            pltpu.VMEM((128, 3, 8, 128), BF), pltpu.VMEM((1024, n), BF), pltpu.VMEM((KEPT, 3, 128, n), F32),
         ] + [pltpu.SemaphoreType.DMA] * 9,
         compiler_params=pltpu.CompilerParams(vmem_limit_bytes=60 << 20, collective_id=0, has_side_effects=True),
         name="pointwise",

time: 73.5 us -> 71.3 us (0.970)
  Pallas kernels: 71.5 us -> 69.8 us
    pallas_call x1, Pallas kernels: 63.6 us -> 62 us  [pointwise(): pl.pallas_call(pointwise_kernel, out_shape=(points, points, jax.ShapeDtyp...]
where the time goes in v5:
time: 71.3 us; the launch traced here: 70.6 us
  Pallas kernels  69.8 us (98%)
  between operations  0.8 us (1%)
    pallas_call x1, Pallas kernels, pointwise(): pl.pallas_call(pointwise_kernel, out_shape=(points, points, jax.ShapeDtyp...  62 us
    pallas_call x1, Pallas kernels, callE(): pl.pallas_call(kernelE, out_shape=(point, point, jax.ShapeDtypeStruct((3,...  7.87 us

profile of v5, /device:TPU:7, one launch (start us, length us, event | category | flops | bytes accessed | tf_op | source)
XLA Modules:
  0.0 70.6 jit_solution(9451885661481287648)
XLA Ops:
  0.6 62.0 %pointwise.1 = (bf16[162,2304]{1,0:T(8,128)(2,1)}, bf16[162,2304]{1,0:T(8,128)(2,1)}, bf16[96,2304]{1,0:T(8,128)(2,1)}, bf16[96,768]{1,0:T(8,128)(2,1)}, bf16[96,768]{1,0:T(8,128)(2,1)}) custom-call(bf16[162,2304]{1,0:T(8,128)(2,1)} %x_ref.1, bf16[162,2304]{1,0:T(8,128)(2,1)} %v_ref.1, s32[2,2304]{1,0:T(2,128)} %pm_ref.1, s32[2,2304]{1,0:T(2,128)} %bm_ref.1, ...), custom_call_target="tpu_custom_call" | custom-call | tf_op jit(solution)/shard_map/pointwise/pallas_call | solution.py:258
  62.6 7.9 %project.1 = (bf16[162,2304]{1,0:T(8,128)(2,1)}, bf16[162,2304]{1,0:T(8,128)(2,1)}, f32[3,29241]{1,0:T(4,128)}) custom-call(bf16[162,2304]{1,0:T(8,128)(2,1)} %get-tuple-element.8.s_in, bf16[162,2304]{1,0:T(8,128)(2,1)} %get-tuple-element.9.r_in, bf16[96,768]{1,0:T(8,128)(2,1)} %get-tuple-element.10.L, bf16[96,2304]{1,0:T(8,128)(2,1)} %get-tuple-element.11.O, ...), custom_call_target="tpu_custom_call" | custom-call | tf_op jit(solution)/shard_map/project/pallas_call | solution.py:360

commit v6 on v5

--- a/solution.py
+++ b/solution.py
@@ -12,9 +12,9 @@
 def dot(a,b): return jnp.dot(a,b,preferred_element_type=F32)
 def dot_nt(a,b): return lax.dot_general(a,b,(((1,),(1,)),((),())),preferred_element_type=F32)
 MESH=pl.DeviceIdType.MESH
-EARLY=17
-KEPT=7
-U=1
+EARLY=18
+KEPT=6
+U=3
 REMOTE=True
 
 
@@ -27,9 +27,16 @@
 
 
 def pointwise_kernel(x_ref, v_ref, pm_ref, bm_ref, conn_ref, dens_ref, win_ref, bin_ref, wmid_ref, bmid_ref, wout_ref, grad_ref,
-                     s_out, r_out, grid_ref, left_ref, right_ref, s_ref, r_ref, x16, oo, bias, win2, wmid2, wback2, wt2, send,
-                     recv_ref, pick, keep, send_sem, recv_sem, own_sem, s_sem, r_sem, left_send, left_recv, right_send, right_recv):
+                     s_out, r_out, grid_ref, left_ref, right_ref, s_ref, r_ref, nodes, x16, oo, bias, win2, wmid2, wback2, wt2, send,
+                     recv_ref, pick, keep, send_sem, recv_sem, own_sem, s_sem, r_sem, left_send, left_recv, right_send, right_recv,
+                     x_sem, v_sem, node_sem):
     n = x_ref.shape[1]
+    x_copy = pltpu.make_async_copy(x_ref, s_ref, x_sem)
+    v_copy = pltpu.make_async_copy(v_ref, r_ref, v_sem)
+    node_copy = pltpu.make_async_copy(conn_ref.at[pl.ds(0, 8)], nodes, node_sem)
+    x_copy.start()
+    v_copy.start()
+    node_copy.start()
     if REMOTE:
         nb, nd = lax.axis_size("brick"), lax.axis_size("dom")
         devices = nb * nd
@@ -62,9 +69,11 @@
     first, place = lax.shift_right_logical(r, 4) * 6, r & 15
     selx = ones_where((c == first + place) & (place < 6))
     selv = ones_where((c == first + place - 8) & (place >= 8) & (place < 14))
+    x_copy.wait()
+    v_copy.wait()
     for k in range(0, n, 768):
         sl = slice(k, k + 768)
-        x16[:, sl] = (dot(selx, x_ref[:, sl]) + dot(selv, v_ref[:, sl])).astype(BF)
+        x16[:, sl] = (dot(selx, s_ref[:, sl]) + dot(selv, r_ref[:, sl])).astype(BF)
 
     def column(k):
         return jnp.concatenate([bias[k]] * (n // 128), 1)
@@ -171,7 +180,8 @@
     r_copy = pltpu.make_async_copy(r_ref, r_out, r_sem)
     r_copy.start()
 
-    node = jnp.floor((conn_ref[0:1, :].astype(F32) + 0.5) * (1.0 / 3.0))
+    node_copy.wait()
+    node = jnp.floor((nodes[0:1, :].astype(F32) + 0.5) * (1.0 / 3.0))
     along = jnp.floor((node + 0.5) * (1.0 / 513.0))
     across = (node - along * 513.0) * 0.5
     half = jnp.where(across >= 128.0, 1.0, 0.0)
@@ -258,14 +268,14 @@
     return pl.pallas_call(
         pointwise_kernel,
         out_shape=(points, points, jax.ShapeDtypeStruct((96, n), BF), halo, halo),
-        in_specs=[vmem] * 12,
+        in_specs=[anywhere] * 2 + [vmem] * 2 + [anywhere] + [vmem] * 7,
         out_specs=(anywhere,) * 2 + (vmem,) * 3,
         scratch_shapes=[
-            pltpu.VMEM((162, n), BF), pltpu.VMEM((162, n), BF),
+            pltpu.VMEM((162, n), BF), pltpu.VMEM((162, n), BF), pltpu.VMEM((8, n), jnp.int32),
             pltpu.VMEM((432, n), BF), pltpu.VMEM((432, n), F32), pltpu.VMEM((3, 128, 128), F32), pltpu.VMEM((256, 16), BF),
             pltpu.VMEM((256, 256), BF), pltpu.VMEM((256, 256), BF), pltpu.VMEM((16, 256), BF), pltpu.VMEM((128, 3, 8, 128), BF),
             pltpu.VMEM((128, 3, 8, 128), BF), pltpu.VMEM((1024, n), BF), pltpu.VMEM((KEPT, 3, 128, n), F32),
-        ] + [pltpu.SemaphoreType.DMA] * 9,
+        ] + [pltpu.SemaphoreType.DMA] * 12,
         compiler_params=pltpu.CompilerParams(vmem_limit_bytes=60 << 20, collective_id=0, has_side_effects=True),
         name="pointwise",
     )(strain, rate, part_map, brick_map, connectivity, density, weight_in.T, row(bias_in), weight_mid, row(bias_mid), row(weight_out),

time: 71.3 us -> 69.5 us (0.975)
  Pallas kernels: 69.8 us -> 68.1 us
    pallas_call x1, Pallas kernels: 62 us -> 60.2 us  [pointwise(): pl.pallas_call(pointwise_kernel, out_shape=(points, points, jax.ShapeDtyp...]
where the time goes in v6:
time: 69.5 us; the launch traced here: 68.9 us
  Pallas kernels  68.1 us (98%)
  between operations  0.84 us (1%)
    pallas_call x1, Pallas kernels, pointwise(): pl.pallas_call(pointwise_kernel, out_shape=(points, points, jax.ShapeDtyp...  60.2 us
    pallas_call x1, Pallas kernels, callE(): pl.pallas_call(kernelE, out_shape=(point, point, jax.ShapeDtypeStruct((3,...  7.89 us

profile of v6, /device:TPU:7, one launch (start us, length us, event | category | flops | bytes accessed | tf_op | source)
XLA Modules:
  0.0 68.9 jit_solution(15803593068701382069)
XLA Ops:
  0.6 60.2 %pointwise.1 = (bf16[162,2304]{1,0:T(8,128)(2,1)}, bf16[162,2304]{1,0:T(8,128)(2,1)}, bf16[96,2304]{1,0:T(8,128)(2,1)}, bf16[96,768]{1,0:T(8,128)(2,1)}, bf16[96,768]{1,0:T(8,128)(2,1)}) custom-call(bf16[162,2304]{1,0:T(8,128)(2,1)} %x_ref.1, bf16[162,2304]{1,0:T(8,128)(2,1)} %v_ref.1, s32[2,2304]{1,0:T(2,128)} %pm_ref.1, s32[2,2304]{1,0:T(2,128)} %bm_ref.1, ...), custom_call_target="tpu_custom_call" | custom-call | tf_op jit(solution)/shard_map/pointwise/pallas_call | solution.py:268
  60.8 7.9 %project.1 = (bf16[162,2304]{1,0:T(8,128)(2,1)}, bf16[162,2304]{1,0:T(8,128)(2,1)}, f32[3,29241]{1,0:T(4,128)}) custom-call(bf16[162,2304]{1,0:T(8,128)(2,1)} %get-tuple-element.8.s_in, bf16[162,2304]{1,0:T(8,128)(2,1)} %get-tuple-element.9.r_in, bf16[96,768]{1,0:T(8,128)(2,1)} %get-tuple-element.10.L, bf16[96,2304]{1,0:T(8,128)(2,1)} %get-tuple-element.11.O, ...), custom_call_target="tpu_custom_call" | custom-call | tf_op jit(solution)/shard_map/project/pallas_call | solution.py:370

commit v7 on v6

--- a/solution.py
+++ b/solution.py
@@ -12,8 +12,8 @@
 def dot(a,b): return jnp.dot(a,b,preferred_element_type=F32)
 def dot_nt(a,b): return lax.dot_general(a,b,(((1,),(1,)),((),())),preferred_element_type=F32)
 MESH=pl.DeviceIdType.MESH
-EARLY=18
-KEPT=6
+EARLY=15
+KEPT=12
 U=3
 REMOTE=True
 
@@ -28,7 +28,7 @@
 
 def pointwise_kernel(x_ref, v_ref, pm_ref, bm_ref, conn_ref, dens_ref, win_ref, bin_ref, wmid_ref, bmid_ref, wout_ref, grad_ref,
                      s_out, r_out, grid_ref, left_ref, right_ref, s_ref, r_ref, nodes, x16, oo, bias, win2, wmid2, wback2, wt2, send,
-                     recv_ref, pick, keep, send_sem, recv_sem, own_sem, s_sem, r_sem, left_send, left_recv, right_send, right_recv,
+                     recv_ref, pick, kept_act, kept, send_sem, recv_sem, own_sem, s_sem, r_sem, left_send, left_recv, right_send, right_recv,
                      x_sem, v_sem, node_sem):
     n = x_ref.shape[1]
     x_copy = pltpu.make_async_copy(x_ref, s_ref, x_sem)
@@ -107,17 +107,17 @@
         grad = column(2) * (1.0 - act2 * act2)
         b1 = dot(wback2[0:128, 0:128], grad.astype(BF))
         oo[group(g), :] = dot(wt2[:, 0:128], ((1.0 - act * act) * b1).astype(BF))
-        keep[g - EARLY, 0] = act
-        keep[g - EARLY, 1] = act2 * grad
-        keep[g - EARLY, 2] = b1
+        kept_act[g - EARLY] = act
+        kept[g - EARLY, 0] = (act2 * grad).astype(BF)
+        kept[g - EARLY, 1] = b1.astype(BF)
 
     def rate(g):
-        act = keep[g - EARLY, 0]
+        act = kept_act[g - EARLY]
         slope = 1.0 - act * act
         tan = slope * dot(win2[128:256], x16[group(g), :])
-        curv = keep[g - EARLY, 1] * dot(wmid2[0:128, 0:128], tan.astype(BF))
+        curv = kept[g - EARLY, 0].astype(F32) * dot(wmid2[0:128, 0:128], tan.astype(BF))
         b2 = dot(wback2[0:128, 0:128], curv.astype(BF))
-        d2 = slope * b2 + act * tan * keep[g - EARLY, 2]
+        d2 = slope * b2 + act * tan * kept[g - EARLY, 1].astype(F32)
         oo[pl.ds(pl.multiple_of(g * 16 + 8, 8), 8), :] = dot(wt2[:, 128:256], d2.astype(BF))[8:16]
 
     def run(body, low, high):
@@ -129,7 +129,8 @@
 
     run(both, 0, EARLY)
     run(value_keep, EARLY, EARLY + KEPT)
-    run(value, EARLY + KEPT, 27)
+    if EARLY + KEPT < 27:
+        run(value, EARLY + KEPT, 27)
 
     r, c = iota((162, 432), 0), iota((162, 432), 1)
     first, place = lax.shift_right_logical(c, 4) * 6, c & 15
@@ -173,7 +174,8 @@
         lax.fori_loop(1, devices, push, 0)
 
     run(rate, EARLY, EARLY + KEPT)
-    run(both, EARLY + KEPT, 27)
+    if EARLY + KEPT < 27:
+        run(both, EARLY + KEPT, 27)
     for k in range(0, n, 768):
         sl = slice(k, k + 768)
         r_ref[:, sl] = dot(pick_r, oo[:, sl].astype(BF)).astype(BF)
@@ -274,7 +276,7 @@
             pltpu.VMEM((162, n), BF), pltpu.VMEM((162, n), BF), pltpu.VMEM((8, n), jnp.int32),
             pltpu.VMEM((432, n), BF), pltpu.VMEM((432, n), F32), pltpu.VMEM((3, 128, 128), F32), pltpu.VMEM((256, 16), BF),
             pltpu.VMEM((256, 256), BF), pltpu.VMEM((256, 256), BF), pltpu.VMEM((16, 256), BF), pltpu.VMEM((128, 3, 8, 128), BF),
-            pltpu.VMEM((128, 3, 8, 128), BF), pltpu.VMEM((1024, n), BF), pltpu.VMEM((KEPT, 3, 128, n), F32),
+            pltpu.VMEM((128, 3, 8, 128), BF), pltpu.VMEM((1024, n), BF), pltpu.VMEM((KEPT, 128, n), F32), pltpu.VMEM((KEPT, 2, 128, n), BF),
         ] + [pltpu.SemaphoreType.DMA] * 12,
         compiler_params=pltpu.CompilerParams(vmem_limit_bytes=60 << 20, collective_id=0, has_side_effects=True),
         name="pointwise",

time: 69.5 us -> 68.1 us (0.980)
  Pallas kernels: 68.1 us -> 66.7 us
    pallas_call x1, Pallas kernels: 60.2 us -> 58.8 us  [pointwise(): pl.pallas_call(pointwise_kernel, out_shape=(points, points, jax.ShapeDtyp...]
where the time goes in v7:
time: 68.1 us; the launch traced here: 67.5 us
  Pallas kernels  66.7 us (98%)
  between operations  0.8 us (1%)
    pallas_call x1, Pallas kernels, pointwise(): pl.pallas_call(pointwise_kernel, out_shape=(points, points, jax.ShapeDtyp...  58.8 us
    pallas_call x1, Pallas kernels, callE(): pl.pallas_call(kernelE, out_shape=(point, point, jax.ShapeDtypeStruct((3,...  7.87 us

profile of v7, /device:TPU:7, one launch (start us, length us, event | category | flops | bytes accessed | tf_op | source)
XLA Modules:
  0.0 67.5 jit_solution(4612206022726328172)
XLA Ops:
  0.6 58.8 %pointwise.1 = (bf16[162,2304]{1,0:T(8,128)(2,1)}, bf16[162,2304]{1,0:T(8,128)(2,1)}, bf16[96,2304]{1,0:T(8,128)(2,1)}, bf16[96,768]{1,0:T(8,128)(2,1)}, bf16[96,768]{1,0:T(8,128)(2,1)}) custom-call(bf16[162,2304]{1,0:T(8,128)(2,1)} %x_ref.1, bf16[162,2304]{1,0:T(8,128)(2,1)} %v_ref.1, s32[2,2304]{1,0:T(2,128)} %pm_ref.1, s32[2,2304]{1,0:T(2,128)} %bm_ref.1, ...), custom_call_target="tpu_custom_call" | custom-call | tf_op jit(solution)/shard_map/pointwise/pallas_call | solution.py:270
  59.5 7.9 %project.1 = (bf16[162,2304]{1,0:T(8,128)(2,1)}, bf16[162,2304]{1,0:T(8,128)(2,1)}, f32[3,29241]{1,0:T(4,128)}) custom-call(bf16[162,2304]{1,0:T(8,128)(2,1)} %get-tuple-element.8.s_in, bf16[162,2304]{1,0:T(8,128)(2,1)} %get-tuple-element.9.r_in, bf16[96,768]{1,0:T(8,128)(2,1)} %get-tuple-element.10.L, bf16[96,2304]{1,0:T(8,128)(2,1)} %get-tuple-element.11.O, ...), custom_call_target="tpu_custom_call" | custom-call | tf_op jit(solution)/shard_map/project/pallas_call | solution.py:372

commit v8 on v7

--- a/solution.py
+++ b/solution.py
@@ -12,8 +12,8 @@
 def dot(a,b): return jnp.dot(a,b,preferred_element_type=F32)
 def dot_nt(a,b): return lax.dot_general(a,b,(((1,),(1,)),((),())),preferred_element_type=F32)
 MESH=pl.DeviceIdType.MESH
-EARLY=15
-KEPT=12
+EARLY=12
+KEPT=15
 U=3
 REMOTE=True
 

time: 68.1 us -> 67.1 us (0.985)
  Pallas kernels: 66.7 us -> 65.1 us
    pallas_call x1, Pallas kernels: 58.8 us -> 57.3 us  [pointwise(): pl.pallas_call(pointwise_kernel, out_shape=(points, points, jax.ShapeDtyp...]
where the time goes in v8:
time: 67.1 us; the launch traced here: 65.9 us
  Pallas kernels  65.1 us (97%)
  between operations  0.8 us (1%)
    pallas_call x1, Pallas kernels, pointwise(): pl.pallas_call(pointwise_kernel, out_shape=(points, points, jax.ShapeDtyp...  57.3 us
    pallas_call x1, Pallas kernels, callE(): pl.pallas_call(kernelE, out_shape=(point, point, jax.ShapeDtypeStruct((3,...  7.87 us

profile of v8, /device:TPU:7, one launch (start us, length us, event | category | flops | bytes accessed | tf_op | source)
XLA Modules:
  0.0 65.9 jit_solution(13384301368106050432)
XLA Ops:
  0.6 57.3 %pointwise.1 = (bf16[162,2304]{1,0:T(8,128)(2,1)}, bf16[162,2304]{1,0:T(8,128)(2,1)}, bf16[96,2304]{1,0:T(8,128)(2,1)}, bf16[96,768]{1,0:T(8,128)(2,1)}, bf16[96,768]{1,0:T(8,128)(2,1)}) custom-call(bf16[162,2304]{1,0:T(8,128)(2,1)} %x_ref.1, bf16[162,2304]{1,0:T(8,128)(2,1)} %v_ref.1, s32[2,2304]{1,0:T(2,128)} %pm_ref.1, s32[2,2304]{1,0:T(2,128)} %bm_ref.1, ...), custom_call_target="tpu_custom_call" | custom-call | tf_op jit(solution)/shard_map/pointwise/pallas_call | solution.py:270
  57.9 7.9 %project.1 = (bf16[162,2304]{1,0:T(8,128)(2,1)}, bf16[162,2304]{1,0:T(8,128)(2,1)}, f32[3,29241]{1,0:T(4,128)}) custom-call(bf16[162,2304]{1,0:T(8,128)(2,1)} %get-tuple-element.8.s_in, bf16[162,2304]{1,0:T(8,128)(2,1)} %get-tuple-element.9.r_in, bf16[96,768]{1,0:T(8,128)(2,1)} %get-tuple-element.10.L, bf16[96,2304]{1,0:T(8,128)(2,1)} %get-tuple-element.11.O, ...), custom_call_target="tpu_custom_call" | custom-call | tf_op jit(solution)/shard_map/project/pallas_call | solution.py:372
